TPU v7x, 32 devices: a whole 2x2x4 slice. The times are simulated.
32 devices in a mesh: dp: 16 (over z, y, x), tensor: 2 (over core).
Axes of the slice: x: 2, y: 2, z: 4, core: 2. Of those that a mesh axis runs over, the one named last changes fastest.
Arguments:
- tokens: bfloat16 [32768, 512], P(('dp', 'tensor')), may hold values from -6 to 6
- block_ids: int32 [32768], P('dp'), may hold values from 0 to 255, never falling along the last dimension, each value on 1 to 256 neighbouring positions
- ln1_gain: bfloat16 [512], P('dp'), may hold values from 0.5 to 1.5
- ln1_bias: bfloat16 [512], P('dp'), may hold values from -1.5 to 1.5
- w_query: bfloat16 [512, 512], P('dp', 'tensor'), may hold values from -0.25 to 0.25
- w_key: bfloat16 [512, 512], P('dp', 'tensor'), may hold values from -0.25 to 0.25
- w_value: bfloat16 [512, 512], P('dp', 'tensor'), may hold values from -0.25 to 0.25
- w_pos: bfloat16 [512, 512], P('dp', 'tensor'), may hold values from -0.25 to 0.25
- bias_u: bfloat16 [512], P('dp'), may hold values from -2.5 to 2.5
- bias_w: bfloat16 [512], P('dp'), may hold values from -2.5 to 2.5
- w_out: bfloat16 [512, 512], P('tensor', 'dp'), may hold values from -1.5 to 1.5
- ln2_gain: bfloat16 [512], P('dp'), may hold values from 0.5 to 1.5
- ln2_bias: bfloat16 [512], P('dp'), may hold values from -1.5 to 1.5
- w_up: bfloat16 [512, 2048], P('dp', 'tensor'), may hold values from -0.25 to 0.25
- bias_up: bfloat16 [2048], P('dp'), may hold values from -1.5 to 1.5
- w_down: bfloat16 [2048, 512], P('tensor', 'dp'), may hold values from -0.125 to 0.125
- bias_down: bfloat16 [512], P('dp'), may hold values from -1.5 to 1.5
- cotangent: bfloat16 [32768, 512], P(('dp', 'tensor')), may hold values from -6 to 6
Outputs:
- output: bfloat16 [32768, 512], P(('dp', 'tensor'))
- grad_tokens: float32 [32768, 512], P(('dp', 'tensor'))
- grad_ln1_gain: float32 [512], P('dp')
- grad_ln1_bias: float32 [512], P('dp')
- grad_w_query: float32 [512, 512], P('dp', 'tensor')
- grad_w_key: float32 [512, 512], P('dp', 'tensor')
- grad_w_value: float32 [512, 512], P('dp', 'tensor')
- grad_w_pos: float32 [512, 512], P('dp', 'tensor')
- grad_bias_u: float32 [512], P('dp')
- grad_bias_w: float32 [512], P('dp')
- grad_w_out: float32 [512, 512], P('tensor', 'dp')
- grad_ln2_gain: float32 [512], P('dp')
- grad_ln2_bias: float32 [512], P('dp')
- grad_w_up: float32 [512, 2048], P('dp', 'tensor')
- grad_bias_up: float32 [2048], P('dp')
- grad_w_down: float32 [2048, 512], P('tensor', 'dp')
- grad_bias_down: float32 [512], P('dp')
Inputs may be any that keep to these rules, and one draw needn't show every extreme that they name: `block_ids`: block ids never fall along the tokens; each block has 1 to 256 tokens, and some block has exactly 256.
All inputs are finite; a program needn't handle non-finite values.
Results may differ from a plain program's by a relative error of at most 0.019.
Values may be sent and summed in bfloat16 or wider, within the bound.
A program may use at most 256 MiB of HBM per device.

v0:
```python
import math

import jax
import jax.numpy as jnp
from jax import lax
from jax.sharding import PartitionSpec as P

D = 512
HEAD = 64
L = 2048
QB = 512


def layer_norm(values, gain_vec, shift_vec):
    center = values - jnp.mean(values, axis=-1, keepdims=True)
    spread = jnp.mean(center * center, axis=-1, keepdims=True)
    return center * lax.rsqrt(spread + 1e-05) * gain_vec + shift_vec


def sinusoid_table(length, table_width):
    distance = (length - 1 - jnp.arange(2 * length - 1, dtype=jnp.int32)).astype(jnp.float32)
    freqs = jnp.exp(
        jnp.arange(0, table_width, 2, dtype=jnp.int32).astype(jnp.float32)
        * (-math.log(10000.0) / table_width)
    )
    angles = distance[:, None] * freqs[None, :]
    return jnp.concatenate([jnp.sin(angles), jnp.cos(angles)], axis=1)


def shift_each_row(table, direction):
    row_count = table.shape[1]
    amount = row_count - 1 - jnp.arange(row_count, dtype=jnp.int32)
    stride = 1
    while stride < row_count:
        picked = (jnp.bitwise_and(amount, stride) != 0)[None, :, None]
        table = jnp.where(picked, jnp.roll(table, direction * stride, axis=2), table)
        stride = stride * 2
    return table


def take_rows(array, first_row, row_count):
    return lax.dynamic_slice_in_dim(array, first_row, row_count, 0)


def take_cols(array, first_col, col_count):
    return lax.dynamic_slice_in_dim(array, first_col, col_count, array.ndim - 1)


def contract_rows(left, right):
    return lax.dot_general(
        left, right, (((0,), (0,)), ((), ())), preferred_element_type=jnp.float32
    )


def times_transpose(left, right):
    return lax.dot_general(
        left, right, (((1,), (1,)), ((), ())), preferred_element_type=jnp.float32
    )


def project_cols(weight, row_data):
    return lax.dot_general(
        weight, row_data, (((0,), (1,)), ((), ())), preferred_element_type=jnp.float32
    )


def placed(part_vec, length, offset):
    return lax.dynamic_update_slice_in_dim(jnp.zeros((length,), jnp.float32), part_vec, offset, 0)


def local(
    tokens,
    block_ids,
    ln1_gain,
    ln1_bias,
    w_query,
    w_key,
    w_value,
    w_pos,
    bias_u,
    bias_w,
    w_out,
    ln2_gain,
    ln2_bias,
    w_up,
    bias_up,
    w_down,
    bias_down,
    cotangent,
):
    member = lax.axis_index("tensor")
    gathered = (
        lax.all_gather(ln1_gain, "dp", axis=0, tiled=True),
        lax.all_gather(ln1_bias, "dp", axis=0, tiled=True),
        lax.all_gather(w_query, "dp", axis=0, tiled=True),
        lax.all_gather(w_key, "dp", axis=0, tiled=True),
        lax.all_gather(w_value, "dp", axis=0, tiled=True),
        lax.all_gather(w_pos, "dp", axis=0, tiled=True),
        lax.all_gather(bias_u, "dp", axis=0, tiled=True),
        lax.all_gather(bias_w, "dp", axis=0, tiled=True),
        lax.all_gather(w_out, "dp", axis=1, tiled=True),
        lax.all_gather(ln2_gain, "dp", axis=0, tiled=True),
        lax.all_gather(ln2_bias, "dp", axis=0, tiled=True),
        lax.all_gather(w_up, "dp", axis=0, tiled=True),
        lax.all_gather(bias_up, "dp", axis=0, tiled=True),
        lax.all_gather(w_down, "dp", axis=1, tiled=True),
        lax.all_gather(bias_down, "dp", axis=0, tiled=True),
    )
    (
        gain_one,
        shift_one,
        query_mat,
        key_mat,
        value_mat,
        pos_mat,
        bias_one,
        bias_two,
        out_mat,
        gain_two,
        shift_two,
        up_mat,
        up_shift,
        down_mat,
        down_shift,
    ) = gathered
    gain_one = gain_one.astype(jnp.float32)
    shift_one = shift_one.astype(jnp.float32)
    gain_two = gain_two.astype(jnp.float32)
    shift_two = shift_two.astype(jnp.float32)
    local_width = query_mat.shape[1]
    head_count = local_width // HEAD
    hidden_local = up_mat.shape[1]
    full_hidden = up_shift.shape[0]
    own_u = lax.dynamic_slice_in_dim(
        bias_one.astype(jnp.float32), member * local_width, local_width
    )
    own_w = lax.dynamic_slice_in_dim(
        bias_two.astype(jnp.float32), member * local_width, local_width
    )
    score_scale = 1.0 / math.sqrt(HEAD)
    own_rows = tokens.shape[0]
    inputs = tokens.astype(jnp.float32)
    normed = layer_norm(inputs, gain_one, shift_one)
    rows_all = lax.all_gather(normed.astype(jnp.bfloat16), "tensor", axis=0, tiled=True)
    total_rows = rows_all.shape[0]
    seq_count = total_rows // L
    queries_t = project_cols(query_mat, rows_all)
    query_u = (
        (queries_t + own_u[:, None]).astype(jnp.bfloat16).reshape(head_count, HEAD, total_rows)
    )
    query_w = (
        (queries_t + own_w[:, None]).astype(jnp.bfloat16).reshape(head_count, HEAD, total_rows)
    )
    key_rows = (
        project_cols(key_mat, rows_all).astype(jnp.bfloat16).reshape(head_count, HEAD, total_rows)
    )
    value_rows = (
        project_cols(value_mat, rows_all).astype(jnp.bfloat16).reshape(head_count, HEAD, total_rows)
    )
    sin_table = jnp.concatenate(
        [sinusoid_table(L, D), jnp.zeros((1, D), jnp.float32)], axis=0
    ).astype(jnp.bfloat16)
    rel_keys = (
        project_cols(pos_mat, sin_table).astype(jnp.bfloat16).reshape(head_count, HEAD, 2 * L)
    )

    def block_scores(first_row):
        seq_start = first_row // L * L
        offset = first_row - seq_start
        qu_block = take_cols(query_u, first_row, QB)
        qw_block = take_cols(query_w, first_row, QB)
        key_block = take_cols(key_rows, seq_start, L)
        rel_block = take_cols(rel_keys, L - QB - offset, QB + L)
        content = jnp.einsum(
            "hda,hdj->haj", qu_block, key_block, preferred_element_type=jnp.float32
        )
        position_full = jnp.einsum(
            "hda,hdt->hat", qw_block, rel_block, preferred_element_type=jnp.float32
        )
        position = shift_each_row(position_full, -1)[:, :, :L]
        scores = (content + position) * score_scale
        ids_query = take_rows(block_ids, first_row, QB)
        ids_key = take_rows(block_ids, seq_start, L)
        allowed = ids_key[None, :] <= ids_query[:, None]
        scores = jnp.where(allowed[None], scores, -1e30)
        return (scores, qu_block, qw_block, key_block, rel_block)

    def attend(first_row):
        scores = block_scores(first_row)[0]
        peak_score = jnp.max(scores, axis=-1, keepdims=True)
        attn_probs = jnp.exp(scores - peak_score)
        row_total = jnp.sum(attn_probs, axis=-1, keepdims=True)
        attn_probs = attn_probs / row_total
        value_block = take_cols(value_rows, first_row // L * L, L)
        mixed_heads = jnp.einsum(
            "haj,hdj->hda",
            attn_probs.astype(jnp.bfloat16),
            value_block,
            preferred_element_type=jnp.float32,
        )
        return (
            mixed_heads.reshape(local_width, QB).astype(jnp.bfloat16),
            (peak_score + jnp.log(row_total))[..., 0],
        )

    block_count = total_rows // QB
    starts = jnp.arange(block_count, dtype=jnp.int32) * QB
    mixed_blocks, log_sums = lax.map(attend, starts)
    mixed_cols = jnp.transpose(mixed_blocks, (1, 0, 2)).reshape(local_width, total_rows)
    residual = inputs + lax.psum_scatter(
        contract_rows(
            take_cols(mixed_cols, jnp.int32(0), own_rows * lax.axis_size("tensor")), out_mat
        ).astype(jnp.bfloat16),
        "tensor",
        scatter_dimension=0,
        tiled=True,
    ).astype(jnp.float32)
    normed_two = layer_norm(residual, gain_two, shift_two)
    grad_output = cotangent.astype(jnp.float32)
    grad_down_bias = placed(jnp.sum(grad_output, axis=0), D, 0)
    own_up = lax.dynamic_slice_in_dim(
        up_shift.astype(jnp.float32), member * hidden_local, hidden_local
    )
    rows_two = lax.all_gather(normed_two.astype(jnp.bfloat16), "tensor", axis=0, tiled=True)
    hidden = jnp.dot(rows_two, up_mat, preferred_element_type=jnp.float32) + own_up
    active = jax.nn.gelu(hidden).astype(jnp.bfloat16)
    output = (
        residual
        + lax.psum_scatter(
            jnp.dot(
                take_rows(active, jnp.int32(0), own_rows * lax.axis_size("tensor")),
                down_mat,
                preferred_element_type=jnp.float32,
            ).astype(jnp.bfloat16),
            "tensor",
            scatter_dimension=0,
            tiled=True,
        ).astype(jnp.float32)
        + down_shift.astype(jnp.float32)
    )
    grad_full = lax.all_gather(cotangent, "tensor", axis=0, tiled=True)
    grad_active = times_transpose(grad_full, down_mat)
    grad_down = contract_rows(active, grad_full)
    gelu_back = jax.vjp(jax.nn.gelu, hidden)[1]
    grad_hidden = gelu_back(grad_active)[0].astype(jnp.bfloat16)
    grad_up_bias = placed(
        jnp.sum(grad_hidden, axis=0, dtype=jnp.float32), full_hidden, member * hidden_local
    )
    grad_up = contract_rows(rows_two, grad_hidden)
    grad_normed_two = lax.psum_scatter(
        times_transpose(
            take_rows(grad_hidden, jnp.int32(0), own_rows * lax.axis_size("tensor")), up_mat
        ).astype(jnp.bfloat16),
        "tensor",
        scatter_dimension=0,
        tiled=True,
    ).astype(jnp.float32)
    norm_back_two = jax.vjp(layer_norm, residual, gain_two, shift_two)[1]
    grad_resid_part, grad_gain_two, grad_shift_two = norm_back_two(grad_normed_two)
    grad_residual = grad_output + grad_resid_part
    ffn_terms = (grad_gain_two, grad_shift_two, grad_up, grad_up_bias, grad_down, grad_down_bias)
    grad_att = lax.all_gather(grad_residual.astype(jnp.bfloat16), "tensor", axis=0, tiled=True)
    grad_out_mat = jnp.dot(mixed_cols, grad_att, preferred_element_type=jnp.float32)
    grad_mixed = (
        times_transpose(out_mat, grad_att)
        .astype(jnp.bfloat16)
        .reshape(head_count, HEAD, total_rows)
    )
    per_seq = L // QB
    log_seq = log_sums.reshape(seq_count, per_seq, head_count, QB)

    def sequence_back(seq_index):
        seq_start = seq_index * L
        log_here = lax.dynamic_index_in_dim(log_seq, seq_index, 0, keepdims=False)
        value_block = take_cols(value_rows, seq_start, L)

        def block_back(carried, block_items):
            grad_keys, grad_values, grad_rel = carried
            block_index, log_block = block_items
            first_row = seq_start + block_index * QB
            scores, qu_block, qw_block, key_block, rel_block = block_scores(first_row)
            attn_probs = jnp.exp(scores - log_block[..., None])
            grad_block = take_cols(grad_mixed, first_row, QB)
            grad_values = grad_values + jnp.einsum(
                "haj,hda->hdj",
                attn_probs.astype(jnp.bfloat16),
                grad_block,
                preferred_element_type=jnp.float32,
            )
            grad_probs = jnp.einsum(
                "hda,hdj->haj", grad_block, value_block, preferred_element_type=jnp.float32
            )
            inner_sum = jnp.sum(attn_probs * grad_probs, axis=-1, keepdims=True)
            grad_scores = (attn_probs * (grad_probs - inner_sum) * score_scale).astype(jnp.bfloat16)
            grad_qu = jnp.einsum(
                "haj,hdj->hda", grad_scores, key_block, preferred_element_type=jnp.float32
            )
            grad_keys = grad_keys + jnp.einsum(
                "haj,hda->hdj", grad_scores, qu_block, preferred_element_type=jnp.float32
            )
            grad_table = shift_each_row(jnp.pad(grad_scores, ((0, 0), (0, 0), (0, QB))), 1)
            grad_qw = jnp.einsum(
                "hat,hdt->hda", grad_table, rel_block, preferred_element_type=jnp.float32
            )
            grad_rel_block = jnp.einsum(
                "hat,hda->hdt", grad_table, qw_block, preferred_element_type=jnp.float32
            )
            col_zero = L - QB - block_index * QB
            grad_rel = lax.dynamic_update_slice_in_dim(
                grad_rel, take_cols(grad_rel, col_zero, QB + L) + grad_rel_block, col_zero, 2
            )
            return ((grad_keys, grad_values, grad_rel), (grad_qu, grad_qw))

        start_carry = (
            jnp.zeros((head_count, HEAD, L), jnp.float32),
            jnp.zeros((head_count, HEAD, L), jnp.float32),
            jnp.zeros((head_count, HEAD, 2 * L), jnp.float32),
        )
        finals, (grad_qu_blocks, grad_qw_blocks) = lax.scan(
            block_back, start_carry, (jnp.arange(per_seq, dtype=jnp.int32), log_here)
        )
        keys_low = finals[0].reshape(local_width, L).astype(jnp.bfloat16)
        values_low = finals[1].reshape(local_width, L).astype(jnp.bfloat16)
        rel_low = finals[2].reshape(local_width, 2 * L).astype(jnp.bfloat16)
        grad_pos_seq = times_transpose(sin_table.T, rel_low)
        qu_cols = jnp.transpose(grad_qu_blocks, (1, 2, 0, 3)).reshape(local_width, L)
        qw_cols = jnp.transpose(grad_qw_blocks, (1, 2, 0, 3)).reshape(local_width, L)
        return (keys_low, values_low, grad_pos_seq, qu_cols, qw_cols)

    seq_results = lax.map(sequence_back, jnp.arange(seq_count, dtype=jnp.int32))

    def join_cols(stacked):
        return jnp.transpose(stacked, (1, 0, 2)).reshape(local_width, total_rows)

    grad_keys_all = join_cols(seq_results[0])
    grad_values_all = join_cols(seq_results[1])
    grad_pos = jnp.sum(seq_results[2], axis=0)
    grad_query_u = join_cols(seq_results[3])
    grad_query_w = join_cols(seq_results[4])
    grad_bias_one = placed(jnp.sum(grad_query_u, axis=1), D, member * local_width)
    grad_bias_two = placed(jnp.sum(grad_query_w, axis=1), D, member * local_width)
    grad_query = (grad_query_u + grad_query_w).astype(jnp.bfloat16)
    grad_query_mat = times_transpose(rows_all.T, grad_query)
    grad_key_mat = times_transpose(rows_all.T, grad_keys_all)
    grad_value_mat = times_transpose(rows_all.T, grad_values_all)
    first_row = jnp.int32(0)
    part_sum = times_transpose(
        take_cols(grad_query, first_row, own_rows * lax.axis_size("tensor")).T, query_mat
    )
    part_sum = part_sum + times_transpose(
        take_cols(grad_keys_all, first_row, own_rows * lax.axis_size("tensor")).T, key_mat
    )
    grad_normed = lax.psum_scatter(
        (
            part_sum
            + times_transpose(
                take_cols(grad_values_all, first_row, own_rows * lax.axis_size("tensor")).T,
                value_mat,
            )
        ).astype(jnp.bfloat16),
        "tensor",
        scatter_dimension=0,
        tiled=True,
    ).astype(jnp.float32)
    norm_back_one = jax.vjp(layer_norm, inputs, gain_one, shift_one)[1]
    grad_in_part, grad_gain_one, grad_shift_one = norm_back_one(grad_normed)
    grad_tokens = grad_residual + grad_in_part
    shards = (
        lax.psum_scatter(grad_gain_one, "dp", scatter_dimension=0, tiled=True),
        lax.psum_scatter(grad_shift_one, "dp", scatter_dimension=0, tiled=True),
        lax.psum_scatter(grad_query_mat, "dp", scatter_dimension=0, tiled=True),
        lax.psum_scatter(grad_key_mat, "dp", scatter_dimension=0, tiled=True),
        lax.psum_scatter(grad_value_mat, "dp", scatter_dimension=0, tiled=True),
        lax.psum_scatter(grad_pos, "dp", scatter_dimension=0, tiled=True),
        lax.psum_scatter(grad_bias_one, "dp", scatter_dimension=0, tiled=True),
        lax.psum_scatter(grad_bias_two, "dp", scatter_dimension=0, tiled=True),
        lax.psum_scatter(grad_out_mat, "dp", scatter_dimension=1, tiled=True),
        lax.psum_scatter(ffn_terms[0], "dp", scatter_dimension=0, tiled=True),
        lax.psum_scatter(ffn_terms[1], "dp", scatter_dimension=0, tiled=True),
        lax.psum_scatter(ffn_terms[2], "dp", scatter_dimension=0, tiled=True),
        lax.psum_scatter(ffn_terms[3], "dp", scatter_dimension=0, tiled=True),
        lax.psum_scatter(ffn_terms[4], "dp", scatter_dimension=1, tiled=True),
        lax.psum_scatter(ffn_terms[5], "dp", scatter_dimension=0, tiled=True),
    )
    summed = lax.psum(
        (shards[0], shards[1], shards[6], shards[7], shards[9], shards[10], shards[12], shards[14]),
        "tensor",
    )
    return (
        output.astype(jnp.bfloat16),
        grad_tokens,
        summed[0],
        summed[1],
        shards[2],
        shards[3],
        shards[4],
        shards[5],
        summed[2],
        summed[3],
        shards[8],
        summed[4],
        summed[5],
        shards[11],
        summed[6],
        shards[13],
        summed[7],
    )


def solution(mesh):
    in_specs = (
        P(("dp", "tensor"), None),
        P("dp"),
        P("dp"),
        P("dp"),
        P("dp", "tensor"),
        P("dp", "tensor"),
        P("dp", "tensor"),
        P("dp", "tensor"),
        P("dp"),
        P("dp"),
        P("tensor", "dp"),
        P("dp"),
        P("dp"),
        P("dp", "tensor"),
        P("dp"),
        P("tensor", "dp"),
        P("dp"),
        P(("dp", "tensor"), None),
    )
    out_specs = (
        P(("dp", "tensor"), None),
        P(("dp", "tensor"), None),
        P("dp"),
        P("dp"),
        P("dp", "tensor"),
        P("dp", "tensor"),
        P("dp", "tensor"),
        P("dp", "tensor"),
        P("dp"),
        P("dp"),
        P("tensor", "dp"),
        P("dp"),
        P("dp"),
        P("dp", "tensor"),
        P("dp"),
        P("tensor", "dp"),
        P("dp"),
    )
    return jax.shard_map(local, mesh=mesh, in_specs=in_specs, out_specs=out_specs, check_vma=False)
```

profile of v0, /device:TPU:0, one launch (start us, length us, event | category | flops | bytes accessed | tf_op | source)
XLA Modules:
  0.0 4347.9 jit_solution(3890872747231420444)
XLA Ops:
  16.0 44.5 %all-reduce.20 = (bf16[512]{0:T(512)(128)(2,1)S(1)}, bf16[512]{0:T(512)(128)(2,1)S(1)}, bf16[512]{0:T(512)(128)(2,1)S(1)}, bf16[512]{0:T(512)(128)(2,1)S(1)}, bf...) all-reduce(bf16[512]{0:T(512)(128)(2,1)S(1)} %dynamic-update-slice., ...), channel_id=1, replica_groups=mesh['dp'=16,'tensor'=2] {'dp'}, use_global_device_ids=true, to_apply=%add.4 | all-reduce | flops 3584 | bytes 14336
  68.2 37.2 all_gather.60
  105.3 39.3 all_gather.62
  144.8 37.3 all_gather.65
  182.0 41.5 all_gather.66
  223.5 37.2 all_gather.64
  293.6 1379.5 %while.51 = (s32[]{:T(128)}, bf16[4,256,512]{1,2,0:T(8,128)(2,1)}, f32[4,4,512]{2,1,0:T(4,128)}, s32[2048]{0:T(1024)}, s32[4]{0:T(128)}, /*index=5*/bf16[4,64,20...) while((s32[]{:T(128)}, bf16[4,256,512]{1,2,0:T(8,128)(2,1)}, ...), condition=%wide.region_5.6_spmd, body=%wide.region_2.5_spmd.sunk | while | flops 1876043264 | bytes 1498545920 | solution.py:208
  385.5 19.7 slice.565
  423.1 19.7 slice.567
  460.8 19.7 slice.569
  498.5 19.7 slice.571
  536.1 19.7 slice.573
  616.4 19.2 fusion.193
  725.5 19.7 slice.565
  763.1 19.7 slice.567
  800.8 19.7 slice.569
  838.5 19.7 slice.571
  876.1 19.7 slice.573
  956.4 19.2 fusion.193
  1065.5 19.7 slice.565
  1103.1 19.7 slice.567
  1140.8 19.7 slice.569
  1178.5 19.7 slice.571
  1216.1 19.7 slice.573
  1296.4 19.3 fusion.193
  1405.6 19.7 slice.565
  1443.2 19.7 slice.567
  1480.9 19.7 slice.569
  1518.6 19.7 slice.571
  1556.2 19.7 slice.573
  1636.5 19.1 fusion.193
  1691.8 40.7 all-gather
  1755.2 49.1 %all-gather.14.cloned.1.call-done = bf16[1024,512]{0,1:T(8,128)(2,1)} async-done(((bf16[1024,32]{0,1:T(8,128)(2,1)}), bf16[1024,512]{0,1:T(8,128)(2,1)}) %all-gather.14.cloned.1.call-update) | async-done | bytes 1048592 | tf_op jit(solution)/shard_map/all_gather | solution.py:106
  1880.2 1897.2 %while.52 = (s32[]{:T(128)}, f32[4,64,2048]{2,1,0:T(8,128)}, f32[4,64,2048]{2,1,0:T(8,128)}, f32[4,64,4096]{2,1,0:T(8,128)}, f32[4,4,64,512]{3,2,1,0:T(8,128)}, ...) while((s32[]{:T(128)}, f32[4,64,2048]{2,1,0:T(8,128)}, ...), condition=%wide.region_15.16_spmd.clone, body=%wide.region_13.15_spmd.clone.sunk | while | flops 5613698560 | bytes 2054024960 | solution.py:319
  1950.9 19.7 slice.585
  1988.6 19.7 slice.587
  2026.2 19.7 slice.589
  2063.9 19.9 slice.591
  2101.3 19.7 slice.593
  2422.6 19.7 slice.585
  2460.2 19.7 slice.587
  2497.9 19.7 slice.589
  2535.5 20.2 slice.591
  2573.2 19.7 slice.593
  2649.9 18.6 fusion.215
  2895.1 19.7 slice.585
  2932.7 19.7 slice.587
  2970.4 19.7 slice.589
  3008.1 19.9 slice.591
  3045.5 19.7 slice.593
  3122.1 18.6 fusion.215
  3367.6 19.7 slice.585
  3405.3 19.7 slice.587
  3442.9 19.7 slice.589
  3480.6 19.9 slice.591
  3518.0 19.7 slice.593
  3594.6 18.6 fusion.215
  3829.3 77.3 %all-reduce.18 = (f32[512]{0:T(512)S(1)}, f32[512]{0:T(512)S(1)}, f32[512]{0:T(512)S(1)}, f32[512]{0:T(512)S(1)}, f32[512]{0:T(512)S(1)}, /*index=5*/f32[512]{0:T(512)S(1)}, f32[2048]{0:T(1024)S(1)}, f32[512]{0:T(512)S(1)}) all-reduce(f32[512]{0:T(512)S(1)} %get-tuple-element.491, ...), channel_id=6, replica_groups=mesh['dp'=16,'tensor'=2] {'dp'}, use_global_device_ids=true, to_apply=%region_20.21.clone | all-reduce | flops 5632 | bytes 45056
  3910.2 50.9 %reduce-scatter.30.cloned.1.call-done = f32[32,1024]{1,0:T(8,128)} async-done(((f32[512,1024]{1,0:T(8,128)}), f32[32,1024]{1,0:T(8,128)}) %reduce-scatter.30.cloned.1.call-update) | async-done | bytes 131088 | tf_op jit(solution)/shard_map/reduce_scatter | solution.py:380
  3961.1 76.4 %reduce-scatter.28.cloned.1.call-done = f32[256,32]{0,1:T(8,128)} async-done(((f32[256,512]{0,1:T(8,128)}), f32[256,32]{0,1:T(8,128)}) %reduce-scatter.28.cloned.1.call-update) | async-done | bytes 32784 | tf_op jit(solution)/shard_map/reduce_scatter | solution.py:377
  4037.5 75.8 %reduce-scatter.20.cloned.1.call-done = f32[32,256]{1,0:T(8,128)} async-done(((f32[512,256]{1,0:T(8,128)}), f32[32,256]{1,0:T(8,128)}) %reduce-scatter.20.cloned.1.call-update) | async-done | bytes 32784 | tf_op jit(solution)/shard_map/reduce_scatter | solution.py:371
  4113.3 75.6 %reduce-scatter.22.cloned.1.call-done = f32[32,256]{1,0:T(8,128)} async-done(((f32[512,256]{1,0:T(8,128)}), f32[32,256]{1,0:T(8,128)}) %reduce-scatter.22.cloned.1.call-update) | async-done | bytes 32784 | tf_op jit(solution)/shard_map/reduce_scatter | solution.py:372
  4188.9 75.8 %reduce-scatter.24.cloned.1.call-done = f32[32,256]{1,0:T(8,128)} async-done(((f32[512,256]{1,0:T(8,128)}), f32[32,256]{1,0:T(8,128)}) %reduce-scatter.24.cloned.1.call-update) | async-done | bytes 32784 | tf_op jit(solution)/shard_map/reduce_scatter | solution.py:373
  4264.7 75.6 %reduce-scatter.26.cloned.1.call-done = f32[32,256]{1,0:T(8,128)} async-done(((f32[512,256]{1,0:T(8,128)}), f32[32,256]{1,0:T(8,128)}) %reduce-scatter.26.cloned.1.call-update) | async-done | bytes 32784 | tf_op jit(solution)/shard_map/reduce_scatter | solution.py:374
  (1392 shorter events, 2519.8 us)
Async XLA Ops:
  8.0 275.1 %all-gather.8.cloned.1.call-start = ((), (), s32[]{:S(2)}) async-start(), calls=%async_computation.11 | async-start | bytes 3145728 | tf_op jit(solution)/shard_map/all_gather | solution.py:144
  67.6 1616.4 %reduce-scatter.12.cloned.1.call-start = ((), (), s32[]{:S(2)}) async-start(), calls=%async_computation.12 | async-start | bytes 3145728 | tf_op jit(solution)/shard_map/reduce_scatter | solution.py:210
  105.3 184.5 %copy-start.33 = (bf16[512,256]{1,0:T(8,128)(2,1)}, bf16[512,256]{1,0:T(8,128)(2,1)S(1)}, u32[]{:S(2)}) copy-start(bf16[512,256]{1,0:T(8,128)(2,1)S(1)} %all_gather.60) | copy-start | bytes 786436
  144.6 141.8 %copy-start.26 = (bf16[512,256]{1,0:T(8,128)(2,1)}, bf16[512,256]{1,0:T(8,128)(2,1)S(1)}, u32[]{:S(2)}) copy-start(bf16[512,256]{1,0:T(8,128)(2,1)S(1)} %all_gather.62) | copy-start | bytes 786436
  182.0 101.1 %copy-start.28 = (bf16[512,256]{1,0:T(8,128)(2,1)}, bf16[512,256]{1,0:T(8,128)(2,1)S(1)}, u32[]{:S(2)}) copy-start(bf16[512,256]{1,0:T(8,128)(2,1)S(1)} %all_gather.65) | copy-start | bytes 786436
  293.6 1379.5 %copy-start.30 = (bf16[256,512]{0,1:T(8,128)(2,1)S(1)}, bf16[256,512]{0,1:T(8,128)(2,1)}, u32[]{:S(2)}) copy-start(bf16[256,512]{0,1:T(8,128)(2,1)} %all_gather.66) | copy-start | bytes 786436
  385.5 20.3 slice-start.5
  423.1 20.3 slice-start.11
  460.8 20.3 slice-start.17
  498.4 20.3 slice-start.23
  498.4 20.3 copy-start.63
  536.1 20.3 slice-start.29
  536.1 20.3 copy-start.62
  725.5 20.3 slice-start.5
  763.1 20.3 slice-start.11
  800.8 20.3 slice-start.17
  838.4 20.3 slice-start.23
  838.5 20.3 copy-start.63
  876.1 20.3 slice-start.29
  876.1 20.3 copy-start.62
  1178.4 20.3 slice-start.23
  1178.5 20.3 copy-start.63
  1216.1 20.3 slice-start.29
  1216.1 20.3 copy-start.62
  1518.5 20.3 slice-start.23
  1518.5 20.3 copy-start.63
  1556.2 20.3 slice-start.29
  1556.2 20.3 copy-start.62
  1676.6 56.7 %all-gather.12.cloned.1.call-start = ((), (), s32[]{:S(2)}) async-start(), calls=%async_computation.14 | async-start | bytes 1114112 | tf_op jit(solution)/shard_map/all_gather | solution.py:104
  1677.1 67.5 %all-gather.10.cloned.1.call-start = ((), (), s32[]{:S(2)}) async-start(), calls=%async_computation.13 | async-start | bytes 3145728 | tf_op jit(solution)/shard_map/all_gather | solution.py:224
  1690.4 113.9 %all-gather.14.cloned.1.call-start = ((), (), s32[]{:S(2)}) async-start(), calls=%async_computation.15 | async-start | bytes 1114112 | tf_op jit(solution)/shard_map/all_gather | solution.py:106
  1691.0 124.3 %all-gather.16.cloned.1.call-start = ((), (), s32[]{:S(2)}) async-start(), calls=%async_computation.17 | async-start | bytes 3145728 | tf_op jit(solution)/shard_map/all_gather | solution.py:241
  1691.7 151.3 %reduce-scatter.16.cloned.1.call-start = ((), (), s32[]{:S(2)}) async-start(), calls=%async_computation.18 | async-start | bytes 3145728 | tf_op jit(solution)/shard_map/reduce_scatter | solution.py:250
  1832.1 23.9 reduce-scatter.14.cloned.1.call-start
  1838.6 22.2 copy-start.22
  1838.6 35.3 all-gather.18.cloned.1.call-start
  1862.1 1959.3 %reduce-scatter.18.cloned.1.call-start = ((), (), s32[]{:S(2)}) async-start(), calls=%async_computation.20 | async-start | bytes 3145728 | tf_op jit(solution)/shard_map/reduce_scatter | solution.py:353
  1883.9 162.1 %copy-start.44 = (pred[512]{0:T(512)(128)(4,1)}, pred[512]{0:T(512)(128)(4,1)S(1)}, u32[]{:S(2)}) copy-start(pred[512]{0:T(512)(128)(4,1)S(1)} %get-tuple-element.789) | copy-start | bytes 1540 | tf_op jit(solution)/shard_map/while/body/eval_jaxpr/while
  1883.9 86.8 %copy-start.48 = (pred[512]{0:T(512)(128)(4,1)}, pred[512]{0:T(512)(128)(4,1)S(1)}, u32[]{:S(2)}) copy-start(pred[512]{0:T(512)(128)(4,1)S(1)} %get-tuple-element.787) | copy-start | bytes 1540 | tf_op jit(solution)/shard_map/while/body/eval_jaxpr/while
  1883.9 124.4 %copy-start.46 = (pred[512]{0:T(512)(128)(4,1)}, pred[512]{0:T(512)(128)(4,1)S(1)}, u32[]{:S(2)}) copy-start(pred[512]{0:T(512)(128)(4,1)S(1)} %get-tuple-element.788) | copy-start | bytes 1540 | tf_op jit(solution)/shard_map/while/body/eval_jaxpr/while
  1883.9 25.7 copy-start.53
  1883.9 49.6 %copy-start.50 = (pred[512]{0:T(512)(128)(4,1)}, pred[512]{0:T(512)(128)(4,1)S(1)}, u32[]{:S(2)}) copy-start(pred[512]{0:T(512)(128)(4,1)S(1)} %get-tuple-element.786) | copy-start | bytes 1540 | tf_op jit(solution)/shard_map/while/body/eval_jaxpr/while
  2355.7 161.9 %copy-start.44 = (pred[512]{0:T(512)(128)(4,1)}, pred[512]{0:T(512)(128)(4,1)S(1)}, u32[]{:S(2)}) copy-start(pred[512]{0:T(512)(128)(4,1)S(1)} %get-tuple-element.789) | copy-start | bytes 1540 | tf_op jit(solution)/shard_map/while/body/eval_jaxpr/while
  2355.7 86.6 %copy-start.48 = (pred[512]{0:T(512)(128)(4,1)}, pred[512]{0:T(512)(128)(4,1)S(1)}, u32[]{:S(2)}) copy-start(pred[512]{0:T(512)(128)(4,1)S(1)} %get-tuple-element.787) | copy-start | bytes 1540 | tf_op jit(solution)/shard_map/while/body/eval_jaxpr/while
  2355.7 124.2 %copy-start.46 = (pred[512]{0:T(512)(128)(4,1)}, pred[512]{0:T(512)(128)(4,1)S(1)}, u32[]{:S(2)}) copy-start(pred[512]{0:T(512)(128)(4,1)S(1)} %get-tuple-element.788) | copy-start | bytes 1540 | tf_op jit(solution)/shard_map/while/body/eval_jaxpr/while
  2355.7 25.5 copy-start.53
  2355.7 49.4 %copy-start.50 = (pred[512]{0:T(512)(128)(4,1)}, pred[512]{0:T(512)(128)(4,1)S(1)}, u32[]{:S(2)}) copy-start(pred[512]{0:T(512)(128)(4,1)S(1)} %get-tuple-element.786) | copy-start | bytes 1540 | tf_op jit(solution)/shard_map/while/body/eval_jaxpr/while
  2828.2 161.9 %copy-start.44 = (pred[512]{0:T(512)(128)(4,1)}, pred[512]{0:T(512)(128)(4,1)S(1)}, u32[]{:S(2)}) copy-start(pred[512]{0:T(512)(128)(4,1)S(1)} %get-tuple-element.789) | copy-start | bytes 1540 | tf_op jit(solution)/shard_map/while/body/eval_jaxpr/while
  2828.2 86.6 %copy-start.48 = (pred[512]{0:T(512)(128)(4,1)}, pred[512]{0:T(512)(128)(4,1)S(1)}, u32[]{:S(2)}) copy-start(pred[512]{0:T(512)(128)(4,1)S(1)} %get-tuple-element.787) | copy-start | bytes 1540 | tf_op jit(solution)/shard_map/while/body/eval_jaxpr/while
  2828.2 124.2 %copy-start.46 = (pred[512]{0:T(512)(128)(4,1)}, pred[512]{0:T(512)(128)(4,1)S(1)}, u32[]{:S(2)}) copy-start(pred[512]{0:T(512)(128)(4,1)S(1)} %get-tuple-element.788) | copy-start | bytes 1540 | tf_op jit(solution)/shard_map/while/body/eval_jaxpr/while
  2828.3 25.5 copy-start.53
  2828.3 49.4 %copy-start.50 = (pred[512]{0:T(512)(128)(4,1)}, pred[512]{0:T(512)(128)(4,1)S(1)}, u32[]{:S(2)}) copy-start(pred[512]{0:T(512)(128)(4,1)S(1)} %get-tuple-element.786) | copy-start | bytes 1540 | tf_op jit(solution)/shard_map/while/body/eval_jaxpr/while
  3300.5 162.1 %copy-start.44 = (pred[512]{0:T(512)(128)(4,1)}, pred[512]{0:T(512)(128)(4,1)S(1)}, u32[]{:S(2)}) copy-start(pred[512]{0:T(512)(128)(4,1)S(1)} %get-tuple-element.789) | copy-start | bytes 1540 | tf_op jit(solution)/shard_map/while/body/eval_jaxpr/while
  3300.6 86.8 %copy-start.48 = (pred[512]{0:T(512)(128)(4,1)}, pred[512]{0:T(512)(128)(4,1)S(1)}, u32[]{:S(2)}) copy-start(pred[512]{0:T(512)(128)(4,1)S(1)} %get-tuple-element.787) | copy-start | bytes 1540 | tf_op jit(solution)/shard_map/while/body/eval_jaxpr/while
  3300.6 124.4 %copy-start.46 = (pred[512]{0:T(512)(128)(4,1)}, pred[512]{0:T(512)(128)(4,1)S(1)}, u32[]{:S(2)}) copy-start(pred[512]{0:T(512)(128)(4,1)S(1)} %get-tuple-element.788) | copy-start | bytes 1540 | tf_op jit(solution)/shard_map/while/body/eval_jaxpr/while
  3300.6 25.7 copy-start.53
  3300.6 49.6 %copy-start.50 = (pred[512]{0:T(512)(128)(4,1)}, pred[512]{0:T(512)(128)(4,1)S(1)}, u32[]{:S(2)}) copy-start(pred[512]{0:T(512)(128)(4,1)S(1)} %get-tuple-element.786) | copy-start | bytes 1540 | tf_op jit(solution)/shard_map/while/body/eval_jaxpr/while
  3785.3 124.9 %reduce-scatter.32.cloned.1.call-start = ((), (), s32[]{:S(2)}) async-start(), calls=%async_computation.27 | async-start | bytes 2228224 | tf_op jit(solution)/shard_map/reduce_scatter | solution.py:382
  3791.3 169.8 %reduce-scatter.30.cloned.1.call-start = ((), (), s32[]{:S(2)}) async-start(), calls=%async_computation.26 | async-start | bytes 2228224 | tf_op jit(solution)/shard_map/reduce_scatter | solution.py:380
  3798.7 238.8 %reduce-scatter.28.cloned.1.call-start = ((), (), s32[]{:S(2)}) async-start(), calls=%async_computation.25 | async-start | bytes 557056 | tf_op jit(solution)/shard_map/reduce_scatter | solution.py:377
  3802.4 310.9 %reduce-scatter.20.cloned.1.call-start = ((), (), s32[]{:S(2)}) async-start(), calls=%async_computation.21 | async-start | bytes 557056 | tf_op jit(solution)/shard_map/reduce_scatter | solution.py:371
  3805.3 383.6 %reduce-scatter.22.cloned.1.call-start = ((), (), s32[]{:S(2)}) async-start(), calls=%async_computation.22 | async-start | bytes 557056 | tf_op jit(solution)/shard_map/reduce_scatter | solution.py:372
  3806.9 457.8 %reduce-scatter.24.cloned.1.call-start = ((), (), s32[]{:S(2)}) async-start(), calls=%async_computation.23 | async-start | bytes 557056 | tf_op jit(solution)/shard_map/reduce_scatter | solution.py:373
  3809.8 530.5 %reduce-scatter.26.cloned.1.call-start = ((), (), s32[]{:S(2)}) async-start(), calls=%async_computation.24 | async-start | bytes 557056 | tf_op jit(solution)/shard_map/reduce_scatter | solution.py:374
  (403 other events, 6111.2 us)
Sparse Core Ops, SparseCore 0:
  67.7 6.4 all-gather.7
  1676.7 7.2 reduce-scatter.11
  1832.2 10.7 reduce-scatter.15
  1845.1 10.7 reduce-scatter.13
Sparse Core Ops, SparseCore 1:
  1680.2 53.0 all-gather.11
  1735.3 9.3 all-gather.9
  1747.7 56.5 all-gather.13
  1805.9 9.3 all-gather.15
  1862.2 11.6 all-gather.17
  3785.4 10.7 reduce-scatter.17
  3798.9 81.7 reduce-scatter.31
  3883.3 77.7 reduce-scatter.29
  3963.8 73.6 reduce-scatter.27
  4040.4 72.8 reduce-scatter.19
  4116.0 72.8 reduce-scatter.21
  4191.8 72.8 reduce-scatter.23
  4267.4 72.8 reduce-scatter.25
where the time goes:
time: 4360 us; the launch traced here: 4350 us
  other arithmetic  1450 us (33%)
  local copies, waits for them, and re-layouts  1420 us (33%)
  waiting for transfers between devices  536 us (12%)
  matrix products  508 us (12%)
  blocking collectives  358 us (8%)
  loops' own time  53.2 us (1%)
    select_n x96, other arithmetic, shift_each_row(): jnp.where(picked, jnp.roll(table, direction * stride, axis=2), table)  1330 us
    slice x248, local copies, waits for them, and re-layouts, shift_each_row(): jnp.roll(table, direction * stride, axis=2)  1250 us
    dot_general x8, matrix products, block_scores(): jnp.einsum('hda,hdj->haj', qu_block, key_block, preferred_element_type=jn...  151 us
    while x704, local copies, waits for them, and re-layouts  130 us
    unnamed x2, blocking collectives  122 us
  transfers between devices with their start and end apart: 17, of which 14 were waited for; matrix products, arithmetic and copies ran while one was open for 2% of the time, Pallas kernels for 0%

commit v1 on v0

--- a/solution.py
+++ b/solution.py
@@ -2,13 +2,16 @@
 
 import jax
 import jax.numpy as jnp
+import ml_dtypes
+import numpy as np
 from jax import lax
+from jax.experimental import pallas as pl
+from jax.experimental.pallas import tpu as pltpu
 from jax.sharding import PartitionSpec as P
 
 D = 512
 HEAD = 64
 L = 2048
-QB = 512
 
 
 def layer_norm(values, gain_vec, shift_vec):
@@ -17,27 +20,6 @@
     return center * lax.rsqrt(spread + 1e-05) * gain_vec + shift_vec
 
 
-def sinusoid_table(length, table_width):
-    distance = (length - 1 - jnp.arange(2 * length - 1, dtype=jnp.int32)).astype(jnp.float32)
-    freqs = jnp.exp(
-        jnp.arange(0, table_width, 2, dtype=jnp.int32).astype(jnp.float32)
-        * (-math.log(10000.0) / table_width)
-    )
-    angles = distance[:, None] * freqs[None, :]
-    return jnp.concatenate([jnp.sin(angles), jnp.cos(angles)], axis=1)
-
-
-def shift_each_row(table, direction):
-    row_count = table.shape[1]
-    amount = row_count - 1 - jnp.arange(row_count, dtype=jnp.int32)
-    stride = 1
-    while stride < row_count:
-        picked = (jnp.bitwise_and(amount, stride) != 0)[None, :, None]
-        table = jnp.where(picked, jnp.roll(table, direction * stride, axis=2), table)
-        stride = stride * 2
-    return table
-
-
 def take_rows(array, first_row, row_count):
     return lax.dynamic_slice_in_dim(array, first_row, row_count, 0)
 
@@ -62,6 +44,129 @@
     return lax.dot_general(
         weight, row_data, (((0,), (1,)), ((), ())), preferred_element_type=jnp.float32
     )
+
+
+TILE = 256
+TILES = L // TILE
+AUG = HEAD + 16
+LOG2E = 1.4426950408889634
+
+
+def tiles_seen(tile):
+    return min(tile + 2, TILES)
+
+
+PACK = [TILE * sum(tiles_seen(t) for t in range(tile)) for tile in range(TILES + 1)]
+
+
+def angle_table():
+    freqs = np.exp(np.arange(0, D, 2, dtype=np.float64) * (-math.log(10000.0) / D))
+    angles = np.arange(L, dtype=np.float64)[:, None] * freqs[None, :]
+    return np.concatenate([np.cos(angles), np.sin(angles)], axis=1).astype(ml_dtypes.bfloat16)
+
+
+def dot_nn(left, right):
+    return jnp.dot(left, right, preferred_element_type=jnp.float32)
+
+
+def attend_kernel(qu_ref, qw_ref, key_ref, value_ref, pos_ref, ids_ref, row_ref, col_ref, e_ref, o_ref):
+    half = D // 2
+    for tile in range(TILES):
+        rows = slice(tile * TILE, (tile + 1) * TILE)
+        width = tiles_seen(tile) * TILE
+        both = contract_rows(qw_ref[:, rows], pos_ref[...])
+        part_a, part_b = both[:, :half], both[:, half:]
+        cos_i = row_ref[rows, :half].astype(jnp.float32)
+        sin_i = row_ref[rows, half:].astype(jnp.float32)
+        turned = jnp.concatenate(
+            [part_a * sin_i + part_b * cos_i, part_b * sin_i - part_a * cos_i], axis=1
+        ).astype(jnp.bfloat16)
+        scores = dot_nn(turned, col_ref[:, :width]) + contract_rows(
+            qu_ref[:, rows], key_ref[:, :width]
+        )
+        ids_row = ids_ref[:, tile * TILE : width]
+        ids_col = jnp.broadcast_to(ids_row[:, :TILE], (8, TILE)).T[:, :1]
+        edge = jnp.where(ids_row <= ids_col, scores[:, tile * TILE :], -1e30)
+        if tile:
+            scores = jnp.concatenate([scores[:, : tile * TILE], edge], axis=1)
+        else:
+            scores = edge
+        peak = jnp.max(scores, axis=1, keepdims=True)
+        weights = jnp.exp2(scores - peak).astype(jnp.bfloat16)
+        e_ref[:, PACK[tile] : PACK[tile + 1]] = weights
+        o_ref[:, rows] = times_transpose(value_ref[:, :width], weights)
+
+
+def attend_back_kernel(
+    e_ref, qu_ref, qw_ref, key_ref, value_ref, pos_ref, aug_ref, scaled_ref, col_ref,
+    dqu_ref, dqw_ref, dk_ref, dv_ref, dpos_ref,
+):
+    half = D // 2
+    dk_ref[...] = jnp.zeros_like(dk_ref)
+    dv_ref[...] = jnp.zeros_like(dv_ref)
+    for tile in range(TILES):
+        rows = slice(tile * TILE, (tile + 1) * TILE)
+        width = tiles_seen(tile) * TILE
+        weights = e_ref[:, PACK[tile] : PACK[tile + 1]]
+        grad_probs = contract_rows(aug_ref[:, rows], value_ref[:, :width])
+        grad_scores = (weights.astype(jnp.float32) * grad_probs).astype(jnp.bfloat16)
+        dv_ref[:, :width] += dot_nn(scaled_ref[:, rows], weights)
+        dk_ref[:, :width] += dot_nn(qu_ref[:, rows], grad_scores)
+        dqu_ref[:, rows] = times_transpose(key_ref[:, :width], grad_scores)
+        turned = times_transpose(col_ref[:, :width], grad_scores)
+        part_c, part_s = turned[:half], turned[half:]
+        cos_i = col_ref[:half, rows].astype(jnp.float32)
+        sin_i = col_ref[half:, rows].astype(jnp.float32)
+        both = jnp.concatenate(
+            [part_c * sin_i - part_s * cos_i, part_c * cos_i + part_s * sin_i], axis=0
+        ).astype(jnp.bfloat16)
+        dqw_ref[:, rows] = dot_nn(pos_ref[...], both)
+        here = times_transpose(qw_ref[:, rows], both)
+        if tile:
+            dpos_ref[...] += here
+        else:
+            dpos_ref[...] = here
+
+
+def per_head(rows, cols):
+    return pl.BlockSpec((None, rows, cols), lambda h: (h, 0, 0))
+
+
+def shared(rows, cols):
+    return pl.BlockSpec((rows, cols), lambda h: (0, 0))
+
+
+def attend_all(qu, qw, keys, values, pos, ids, row_table, col_table):
+    heads = qu.shape[0]
+    f32, bf16 = jnp.float32, jnp.bfloat16
+    return pl.pallas_call(
+        attend_kernel,
+        grid=(heads,),
+        in_specs=[per_head(HEAD, L)] * 3
+        + [per_head(AUG, L), per_head(HEAD, D), shared(1, L), shared(L, D), shared(D, L)],
+        out_specs=[per_head(TILE, PACK[-1]), per_head(AUG, L)],
+        out_shape=[
+            jax.ShapeDtypeStruct((heads, TILE, PACK[-1]), bf16),
+            jax.ShapeDtypeStruct((heads, AUG, L), f32),
+        ],
+        compiler_params=pltpu.CompilerParams(vmem_limit_bytes=56 * 1024 * 1024),
+    )(qu, qw, keys, values, pos, ids, row_table, col_table)
+
+
+def attend_back_all(weights, qu, qw, keys, values, pos, aug, scaled, col_table):
+    heads = qu.shape[0]
+    f32 = jnp.float32
+    return pl.pallas_call(
+        attend_back_kernel,
+        grid=(heads,),
+        in_specs=[per_head(TILE, PACK[-1])]
+        + [per_head(HEAD, L)] * 3
+        + [per_head(AUG, L), per_head(HEAD, D), per_head(AUG, L), per_head(HEAD, L), shared(D, L)],
+        out_specs=[per_head(HEAD, L)] * 4 + [per_head(HEAD, D)],
+        out_shape=[jax.ShapeDtypeStruct((heads, HEAD, L), f32)] * 4
+        + [jax.ShapeDtypeStruct((heads, HEAD, D), f32)],
+        compiler_params=pltpu.CompilerParams(vmem_limit_bytes=56 * 1024 * 1024),
+    )(weights, qu, qw, keys, values, pos, aug, scaled, col_table)
 
 
 def placed(part_vec, length, offset):
@@ -143,70 +248,33 @@
     normed = layer_norm(inputs, gain_one, shift_one)
     rows_all = lax.all_gather(normed.astype(jnp.bfloat16), "tensor", axis=0, tiled=True)
     total_rows = rows_all.shape[0]
-    seq_count = total_rows // L
     queries_t = project_cols(query_mat, rows_all)
-    query_u = (
-        (queries_t + own_u[:, None]).astype(jnp.bfloat16).reshape(head_count, HEAD, total_rows)
-    )
-    query_w = (
-        (queries_t + own_w[:, None]).astype(jnp.bfloat16).reshape(head_count, HEAD, total_rows)
-    )
-    key_rows = (
-        project_cols(key_mat, rows_all).astype(jnp.bfloat16).reshape(head_count, HEAD, total_rows)
-    )
-    value_rows = (
-        project_cols(value_mat, rows_all).astype(jnp.bfloat16).reshape(head_count, HEAD, total_rows)
-    )
-    sin_table = jnp.concatenate(
-        [sinusoid_table(L, D), jnp.zeros((1, D), jnp.float32)], axis=0
-    ).astype(jnp.bfloat16)
-    rel_keys = (
-        project_cols(pos_mat, sin_table).astype(jnp.bfloat16).reshape(head_count, HEAD, 2 * L)
-    )
-
-    def block_scores(first_row):
-        seq_start = first_row // L * L
-        offset = first_row - seq_start
-        qu_block = take_cols(query_u, first_row, QB)
-        qw_block = take_cols(query_w, first_row, QB)
-        key_block = take_cols(key_rows, seq_start, L)
-        rel_block = take_cols(rel_keys, L - QB - offset, QB + L)
-        content = jnp.einsum(
-            "hda,hdj->haj", qu_block, key_block, preferred_element_type=jnp.float32
-        )
-        position_full = jnp.einsum(
-            "hda,hdt->hat", qw_block, rel_block, preferred_element_type=jnp.float32
-        )
-        position = shift_each_row(position_full, -1)[:, :, :L]
-        scores = (content + position) * score_scale
-        ids_query = take_rows(block_ids, first_row, QB)
-        ids_key = take_rows(block_ids, seq_start, L)
-        allowed = ids_key[None, :] <= ids_query[:, None]
-        scores = jnp.where(allowed[None], scores, -1e30)
-        return (scores, qu_block, qw_block, key_block, rel_block)
-
-    def attend(first_row):
-        scores = block_scores(first_row)[0]
-        peak_score = jnp.max(scores, axis=-1, keepdims=True)
-        attn_probs = jnp.exp(scores - peak_score)
-        row_total = jnp.sum(attn_probs, axis=-1, keepdims=True)
-        attn_probs = attn_probs / row_total
-        value_block = take_cols(value_rows, first_row // L * L, L)
-        mixed_heads = jnp.einsum(
-            "haj,hdj->hda",
-            attn_probs.astype(jnp.bfloat16),
-            value_block,
-            preferred_element_type=jnp.float32,
-        )
-        return (
-            mixed_heads.reshape(local_width, QB).astype(jnp.bfloat16),
-            (peak_score + jnp.log(row_total))[..., 0],
-        )
-
-    block_count = total_rows // QB
-    starts = jnp.arange(block_count, dtype=jnp.int32) * QB
-    mixed_blocks, log_sums = lax.map(attend, starts)
-    mixed_cols = jnp.transpose(mixed_blocks, (1, 0, 2)).reshape(local_width, total_rows)
+    def heads_of(array):
+        return array.astype(jnp.bfloat16).reshape(head_count, HEAD, array.shape[-1])
+
+    ids = block_ids.reshape(1, total_rows)
+    sum_u = queries_t + own_u[:, None]
+    sum_w = queries_t + own_w[:, None]
+    fold = score_scale * LOG2E
+    query_u = heads_of(sum_u)
+    query_w = heads_of(sum_w)
+    key_rows = heads_of(project_cols(key_mat, rows_all))
+    ones = jnp.ones((head_count, 2, total_rows), jnp.bfloat16)
+    blank = jnp.zeros((head_count, AUG - HEAD - 2, total_rows), jnp.bfloat16)
+    value_rows = jnp.concatenate(
+        [heads_of(project_cols(value_mat, rows_all)), ones, blank], axis=1
+    )
+    pos_rows = pos_mat.T.reshape(head_count, HEAD, D)
+    table = angle_table()
+    row_table = jnp.asarray(table)
+    col_table = jnp.asarray(np.ascontiguousarray(table.T))
+    weights, mixed_sums = attend_all(
+        heads_of(sum_u * fold), heads_of(sum_w * fold), key_rows, value_rows, pos_rows, ids,
+        row_table, col_table,
+    )
+    inv_total = 1.0 / mixed_sums[:, HEAD : HEAD + 1]
+    mixed_full = mixed_sums[:, :HEAD] * inv_total
+    mixed_cols = mixed_full.reshape(local_width, total_rows).astype(jnp.bfloat16)
     residual = inputs + lax.psum_scatter(
         contract_rows(
             take_cols(mixed_cols, jnp.int32(0), own_rows * lax.axis_size("tensor")), out_mat
@@ -266,77 +334,21 @@
         .astype(jnp.bfloat16)
         .reshape(head_count, HEAD, total_rows)
     )
-    per_seq = L // QB
-    log_seq = log_sums.reshape(seq_count, per_seq, head_count, QB)
-
-    def sequence_back(seq_index):
-        seq_start = seq_index * L
-        log_here = lax.dynamic_index_in_dim(log_seq, seq_index, 0, keepdims=False)
-        value_block = take_cols(value_rows, seq_start, L)
-
-        def block_back(carried, block_items):
-            grad_keys, grad_values, grad_rel = carried
-            block_index, log_block = block_items
-            first_row = seq_start + block_index * QB
-            scores, qu_block, qw_block, key_block, rel_block = block_scores(first_row)
-            attn_probs = jnp.exp(scores - log_block[..., None])
-            grad_block = take_cols(grad_mixed, first_row, QB)
-            grad_values = grad_values + jnp.einsum(
-                "haj,hda->hdj",
-                attn_probs.astype(jnp.bfloat16),
-                grad_block,
-                preferred_element_type=jnp.float32,
-            )
-            grad_probs = jnp.einsum(
-                "hda,hdj->haj", grad_block, value_block, preferred_element_type=jnp.float32
-            )
-            inner_sum = jnp.sum(attn_probs * grad_probs, axis=-1, keepdims=True)
-            grad_scores = (attn_probs * (grad_probs - inner_sum) * score_scale).astype(jnp.bfloat16)
-            grad_qu = jnp.einsum(
-                "haj,hdj->hda", grad_scores, key_block, preferred_element_type=jnp.float32
-            )
-            grad_keys = grad_keys + jnp.einsum(
-                "haj,hda->hdj", grad_scores, qu_block, preferred_element_type=jnp.float32
-            )
-            grad_table = shift_each_row(jnp.pad(grad_scores, ((0, 0), (0, 0), (0, QB))), 1)
-            grad_qw = jnp.einsum(
-                "hat,hdt->hda", grad_table, rel_block, preferred_element_type=jnp.float32
-            )
-            grad_rel_block = jnp.einsum(
-                "hat,hda->hdt", grad_table, qw_block, preferred_element_type=jnp.float32
-            )
-            col_zero = L - QB - block_index * QB
-            grad_rel = lax.dynamic_update_slice_in_dim(
-                grad_rel, take_cols(grad_rel, col_zero, QB + L) + grad_rel_block, col_zero, 2
-            )
-            return ((grad_keys, grad_values, grad_rel), (grad_qu, grad_qw))
-
-        start_carry = (
-            jnp.zeros((head_count, HEAD, L), jnp.float32),
-            jnp.zeros((head_count, HEAD, L), jnp.float32),
-            jnp.zeros((head_count, HEAD, 2 * L), jnp.float32),
-        )
-        finals, (grad_qu_blocks, grad_qw_blocks) = lax.scan(
-            block_back, start_carry, (jnp.arange(per_seq, dtype=jnp.int32), log_here)
-        )
-        keys_low = finals[0].reshape(local_width, L).astype(jnp.bfloat16)
-        values_low = finals[1].reshape(local_width, L).astype(jnp.bfloat16)
-        rel_low = finals[2].reshape(local_width, 2 * L).astype(jnp.bfloat16)
-        grad_pos_seq = times_transpose(sin_table.T, rel_low)
-        qu_cols = jnp.transpose(grad_qu_blocks, (1, 2, 0, 3)).reshape(local_width, L)
-        qw_cols = jnp.transpose(grad_qw_blocks, (1, 2, 0, 3)).reshape(local_width, L)
-        return (keys_low, values_low, grad_pos_seq, qu_cols, qw_cols)
-
-    seq_results = lax.map(sequence_back, jnp.arange(seq_count, dtype=jnp.int32))
-
-    def join_cols(stacked):
-        return jnp.transpose(stacked, (1, 0, 2)).reshape(local_width, total_rows)
-
-    grad_keys_all = join_cols(seq_results[0])
-    grad_values_all = join_cols(seq_results[1])
-    grad_pos = jnp.sum(seq_results[2], axis=0)
-    grad_query_u = join_cols(seq_results[3])
-    grad_query_w = join_cols(seq_results[4])
+    grad_mixed = grad_mixed.astype(jnp.float32)
+    grad_scaled = (grad_mixed * inv_total).astype(jnp.bfloat16)
+    grad_low = (grad_mixed * (inv_total * score_scale)).astype(jnp.bfloat16)
+    inner = -jnp.sum(grad_low.astype(jnp.float32) * mixed_full, axis=1, keepdims=True)
+    inner_high = inner.astype(jnp.bfloat16)
+    inner_rest = (inner - inner_high.astype(jnp.float32)).astype(jnp.bfloat16)
+    grad_aug = jnp.concatenate([grad_low, inner_high, inner_rest, blank], axis=1)
+    dqu, dqw, dk, dv, dpos = attend_back_all(
+        weights, query_u, query_w, key_rows, value_rows, pos_rows, grad_aug, grad_scaled, col_table
+    )
+    grad_keys_all = dk.reshape(local_width, total_rows).astype(jnp.bfloat16)
+    grad_values_all = dv.reshape(local_width, total_rows).astype(jnp.bfloat16)
+    grad_pos = dpos.reshape(local_width, D).T
+    grad_query_u = dqu.reshape(local_width, total_rows)
+    grad_query_w = dqw.reshape(local_width, total_rows)
     grad_bias_one = placed(jnp.sum(grad_query_u, axis=1), D, member * local_width)
     grad_bias_two = placed(jnp.sum(grad_query_w, axis=1), D, member * local_width)
     grad_query = (grad_query_u + grad_query_w).astype(jnp.bfloat16)

time: 4360 us -> 1150 us (0.26)
  other arithmetic: 1450 us -> 31.8 us
  local copies, waits for them, and re-layouts: 1420 us -> 23.3 us
  matrix products: 508 us -> 70.1 us
  Pallas kernels: 0 us -> 100 us
  loops' own time: 53.2 us -> 0 us
    select_n x96 -> x0, other arithmetic: 1330 us -> none  [shift_each_row(): jnp.where(picked, jnp.roll(table, direction * stride, axis=2), table)]
    slice x248 -> x0, local copies, waits for them, and re-layouts: 1250 us -> none  [shift_each_row(): jnp.roll(table, direction * stride, axis=2)]
    dot_general x40 -> x0, matrix products: 352 us -> none  [the longest x8 151 us: block_scores(): jnp.einsum('hda,hdj->haj', qu_block, key_block, preferred_element_type=jn...]
    while x704 -> x0, local copies, waits for them, and re-layouts: 130 us -> none
    pallas_call x0 -> x2, Pallas kernels: none -> 100 us  [the longest x1 55.6 us: attend_back_all(): pl.pallas_call(attend_back_kernel, grid=(heads,), in_specs=[per_head(TILE...]
    sub x4 -> x0, matrix products: 70.9 us -> none  [block_back(): grad_probs - inner_sum]
    reduce_scatter x1, waiting for transfers between devices: 0.01 us -> 55.6 us  [local(): lax.psum_scatter(ffn_terms[4], 'dp', scatter_dimension=1, tiled=True)]
    another operation x2 -> x0, loops' own time: 53.2 us -> none  [the longest x1 39 us: local(): mixed_blocks, log_sums = lax.map(attend, starts)]
  transfers between devices with their start and end apart: 17 -> 17, of which waited for: 14 -> 14; matrix products, arithmetic and copies ran while one was open for 2% -> 5% of each run, Pallas kernels for 0% -> 0%
where the time goes in v1:
time: 1150 us; the launch traced here: 1140 us
  waiting for transfers between devices  545 us (47%)
  blocking collectives  354 us (31%)
  Pallas kernels  100 us (9%)
  matrix products  70.1 us (6%)
  other arithmetic  31.8 us (3%)
  local copies, waits for them, and re-layouts  23.3 us (2%)
  between operations  18.4 us (2%)
    unnamed x2, blocking collectives  121 us
    reduce_scatter x1, waiting for transfers between devices, local(): lax.psum_scatter(grad_out_mat, 'dp', scatter_dimension=1, tiled=True)  76.6 us
    reduce_scatter x1, waiting for transfers between devices, local(): lax.psum_scatter(grad_query_mat, 'dp', scatter_dimension=0, tiled=True)  75.9 us
    reduce_scatter x1, waiting for transfers between devices, local(): lax.psum_scatter(grad_value_mat, 'dp', scatter_dimension=0, tiled=True)  75.8 us
    reduce_scatter x1, waiting for transfers between devices, local(): lax.psum_scatter(grad_pos, 'dp', scatter_dimension=0, tiled=True)  75.6 us
    reduce_scatter x1, waiting for transfers between devices, local(): lax.psum_scatter(grad_key_mat, 'dp', scatter_dimension=0, tiled=True)  75.6 us
    reduce_scatter x1, waiting for transfers between devices, local(): lax.psum_scatter(ffn_terms[4], 'dp', scatter_dimension=1, tiled=True)  55.6 us
    pallas_call x1, Pallas kernels, attend_back_all(): pl.pallas_call(attend_back_kernel, grid=(heads,), in_specs=[per_head(TILE...  55.6 us
  transfers between devices with their start and end apart: 17, of which 14 were waited for; matrix products, arithmetic and copies ran while one was open for 5% of the time, Pallas kernels for 0%

profile of v1, /device:TPU:0, one launch (start us, length us, event | category | flops | bytes accessed | tf_op | source)
XLA Modules:
  0.0 1144.2 jit_solution(11614928159973452224)
XLA Ops:
  8.1 1.3 fusion.32
  16.0 44.0 %all-reduce.17 = (bf16[512]{0:T(512)(128)(2,1)S(1)}, bf16[512]{0:T(512)(128)(2,1)S(1)}, bf16[512]{0:T(512)(128)(2,1)S(1)}, bf16[512]{0:T(512)(128)(2,1)S(1)}, bf...) all-reduce(bf16[512]{0:T(512)(128)(2,1)S(1)} %dynamic-update-slice., ...), channel_id=1, replica_groups=mesh['dp'=16,'tensor'=2] {'dp'}, use_global_device_ids=true, to_apply=%add.1 | all-reduce | flops 3584 | bytes 14336
  60.1 1.4 convert_reduce_fusion.3
  61.5 1.7 fusion.19
  63.3 1.4 fusion.17
  65.1 36.8 %all_gather.65 = bf16[512,256]{1,0:T(8,128)(2,1)S(1)} all-gather(bf16[32,256]{1,0:T(8,128)(2,1)S(1)} %copy-done.23), channel_id=1, replica_groups=mesh['dp'=16,'tensor'=2] {'dp'}, dimensions={0}, use_global_device_ids=true | all-gather | bytes 278528 | tf_op jit(solution)/shard_map/all_gather | solution.py:203
  102.8 39.1 %all_gather.60 = bf16[512,256]{1,0:T(8,128)(2,1)S(1)} all-gather(bf16[32,256]{1,0:T(8,128)(2,1)S(1)} %copy-done.24), channel_id=1, replica_groups=mesh['dp'=16,'tensor'=2] {'dp'}, dimensions={0}, use_global_device_ids=true | all-gather | bytes 278528 | tf_op jit(solution)/shard_map/all_gather | solution.py:200
  141.9 37.1 %all_gather.64 = bf16[512,256]{1,0:T(8,128)(2,1)S(1)} all-gather(bf16[32,256]{1,0:T(8,128)(2,1)S(1)} %copy-done.25), channel_id=1, replica_groups=mesh['dp'=16,'tensor'=2] {'dp'}, dimensions={0}, use_global_device_ids=true | all-gather | bytes 278528 | tf_op jit(solution)/shard_map/all_gather | solution.py:202
  179.0 38.6 %all_gather.63 = bf16[512,256]{1,0:T(8,128)(2,1)S(1)} all-gather(bf16[32,256]{1,0:T(8,128)(2,1)S(1)} %copy-done.26), channel_id=1, replica_groups=mesh['dp'=16,'tensor'=2] {'dp'}, dimensions={0}, use_global_device_ids=true | all-gather | bytes 278528 | tf_op jit(solution)/shard_map/all_gather | solution.py:201
  217.7 37.2 %all_gather.66 = bf16[256,512]{0,1:T(8,128)(2,1)S(1)} all-gather(bf16[256,32]{0,1:T(8,128)(2,1)S(1)} %copy-done.27), channel_id=1, replica_groups=mesh['dp'=16,'tensor'=2] {'dp'}, dimensions={1}, use_global_device_ids=true | all-gather | bytes 278528 | tf_op jit(solution)/shard_map/all_gather | solution.py:206
  254.9 2.5 convolution_convert_fusion.4
  257.4 1.4 maximum_maximum_fusion.value_ref
  258.8 1.8 convolution_convert_fusion.5
  260.6 3.0 add_convert_fusion.4
  263.5 44.5 %shard_map.323 = (bf16[4,256,11008]{2,1,0:T(8,128)(2,1)}, f32[4,80,2048]{2,1,0:T(8,128)}) custom-call(bf16[4,64,2048]{2,1,0:T(8,128)(2,1)} %bitcast.90, bf16[4,64,2048]{2,1,0:T(8,128)(2,1)} %bitcast.89, bf16[4,64,2048]{2,1,0:T(8,128)(2,1)} %bitcast.77, bf16[4,80,2048]{2,1,0:T(8,128)(2,1)} %maximum_maximum_fusion.value_ref, bf16[4,64,512]{2,1,0:T(8,128)(2,1)} %bitcast.92, ...), custom_call_target="tpu_custom_call" | custom-call | tf_op jit(solution)/shard_map/pallas_call | solution.py:142
  309.0 1.8 fusion.23
  311.8 2.1 convolution_convert_fusion.2
  315.0 6.3 reduce-scatter.12.cloned.1.call-done
  321.3 1.7 fusion.25
  323.5 1.5 add_convert_fusion.3
  326.5 40.7 %all-gather = bf16[16,1,128]{2,1,0:T(2,128)(2,1)S(1)} all-gather(bf16[1,1,128]{2,1,0:T(2,128)(2,1)S(1)} %bitcast.102), channel_id=1, replica_groups=mesh['dp'=16,'tensor'=2] {'dp'}, dimensions={0}, use_global_device_ids=true | all-gather | bytes 4352 | tf_op jit(solution)/shard_map/all_gather | solution.py:210
  367.2 3.4 all-gather.12.cloned.1.call-done
  370.5 11.4 all-gather.10.cloned.1.call-done
  381.9 10.4 multiply_convert_fusion
  392.3 49.2 %all-gather.14.cloned.1.call-done = bf16[1024,512]{0,1:T(8,128)(2,1)} async-done(((bf16[1024,32]{0,1:T(8,128)(2,1)}), bf16[1024,512]{0,1:T(8,128)(2,1)}) %all-gather.14.cloned.1.call-update) | async-done | bytes 1048592 | tf_op jit(solution)/shard_map/all_gather | solution.py:211
  441.5 11.0 all-gather.16.cloned.1.call-done
  452.5 10.2 convert_reduce_fusion
  462.7 2.0 copy-done.32
  464.7 3.8 convolution_convert_fusion
  468.7 6.2 convolution_convert_fusion.1
  475.0 4.5 reduce-scatter.16.cloned.1.call-done
  479.5 2.3 fusion.21
  481.9 10.5 reduce-scatter.14.cloned.1.call-done
  492.4 3.4 fusion.30
  495.8 1.3 copy-done.2
  497.1 1.3 fusion.27
  498.5 11.7 %all-gather.18.cloned.1.call-done = bf16[2048,512]{1,0:T(8,128)(2,1)} async-done(((bf16[1024,512]{1,0:T(8,128)(2,1)}), bf16[2048,512]{1,0:T(8,128)(2,1)}) %all-gather.18.cloned.1.call-update) | async-done | bytes 2097168 | tf_op jit(solution)/shard_map/all_gather | solution.py:330
  510.2 2.5 fusion.11
  512.7 1.6 multiply_reduce_fusion
  514.3 1.5 maximum_maximum_fusion.1.aug_ref
  515.8 55.6 %shard_map.324 = (f32[4,64,2048]{2,1,0:T(8,128)}, f32[4,64,2048]{2,1,0:T(8,128)}, f32[4,64,2048]{2,1,0:T(8,128)}, f32[4,64,2048]{2,1,0:T(8,128)}, f32[4,64,512]{2,1,0:T(8,128)}) custom-call(bf16[4,256,11008]{2,1,0:T(8,128)(2,1)} %get-tuple-element.25.e_ref, bf16[4,64,2048]{2,1,0:T(8,128)(2,1)} %bitcast.88, bf16[4,64,2048]{2,1,0:T(8,128)(2,1)} %bitcast.87, ...), custom_call_target="tpu_custom_call" | custom-call | tf_op jit(solution)/shard_map/pallas_call | solution.py:159
  571.4 1.8 convert_element_type.242
  574.2 1.0 copy-done.21
  579.4 2.1 add_convert_fusion
  581.7 1.3 copy-done.29
  583.0 5.8 fusion.39
  589.0 1.6 copy-done.30
  590.6 6.2 fusion.40
  596.8 3.8 fusion.38
  600.7 2.8 fusion.35
  603.6 2.8 fusion.36
  606.4 2.8 fusion.37
  611.1 2.0 copy.40
  613.6 2.2 convert_reduce_fusion.1
  615.9 2.4 fusion.22
  618.3 2.2 convert_reduce_fusion.4
  620.5 77.4 %all-reduce.15 = (f32[512]{0:T(512)S(1)}, f32[512]{0:T(512)S(1)}, f32[512]{0:T(512)S(1)}, f32[512]{0:T(512)S(1)}, f32[512]{0:T(512)S(1)}, /*index=5*/f32[512]{0:T(512)S(1)}, f32[2048]{0:T(1024)S(1)}, f32[512]{0:T(512)S(1)}) all-reduce(f32[512]{0:T(512)S(1)} %get-tuple-element.33, ...), channel_id=6, replica_groups=mesh['dp'=16,'tensor'=2] {'dp'}, use_global_device_ids=true, to_apply=%region_14.0.clone | all-reduce | flops 5632 | bytes 45056
  698.5 3.0 all-reduce.16
  701.5 55.6 %reduce-scatter.32.cloned.1.call-done = f32[1024,32]{0,1:T(8,128)} async-done(((f32[1024,512]{0,1:T(8,128)}), f32[1024,32]{0,1:T(8,128)}) %reduce-scatter.32.cloned.1.call-update) | async-done | bytes 131088 | tf_op jit(solution)/shard_map/reduce_scatter | solution.py:394
  757.1 76.6 %reduce-scatter.28.cloned.1.call-done = f32[256,32]{0,1:T(8,128)} async-done(((f32[256,512]{0,1:T(8,128)}), f32[256,32]{0,1:T(8,128)}) %reduce-scatter.28.cloned.1.call-update) | async-done | bytes 32784 | tf_op jit(solution)/shard_map/reduce_scatter | solution.py:389
  833.7 75.9 %reduce-scatter.20.cloned.1.call-done = f32[32,256]{1,0:T(8,128)} async-done(((f32[512,256]{1,0:T(8,128)}), f32[32,256]{1,0:T(8,128)}) %reduce-scatter.20.cloned.1.call-update) | async-done | bytes 32784 | tf_op jit(solution)/shard_map/reduce_scatter | solution.py:383
  909.6 75.6 %reduce-scatter.22.cloned.1.call-done = f32[32,256]{1,0:T(8,128)} async-done(((f32[512,256]{1,0:T(8,128)}), f32[32,256]{1,0:T(8,128)}) %reduce-scatter.22.cloned.1.call-update) | async-done | bytes 32784 | tf_op jit(solution)/shard_map/reduce_scatter | solution.py:384
  985.2 75.8 %reduce-scatter.24.cloned.1.call-done = f32[32,256]{1,0:T(8,128)} async-done(((f32[512,256]{1,0:T(8,128)}), f32[32,256]{1,0:T(8,128)}) %reduce-scatter.24.cloned.1.call-update) | async-done | bytes 32784 | tf_op jit(solution)/shard_map/reduce_scatter | solution.py:385
  1061.0 75.6 %reduce-scatter.26.cloned.1.call-done = f32[32,256]{1,0:T(8,128)} async-done(((f32[512,256]{1,0:T(8,128)}), f32[32,256]{1,0:T(8,128)}) %reduce-scatter.26.cloned.1.call-update) | async-done | bytes 32784 | tf_op jit(solution)/shard_map/reduce_scatter | solution.py:386
  (161 shorter events, 20.0 us)
Async XLA Ops:
  8.0 55.2 %copy-start = (bf16[1024,512]{1,0:T(8,128)(2,1)S(1)}, bf16[1024,512]{1,0:T(8,128)(2,1)}, u32[]{:S(2)}) copy-start(bf16[1024,512]{1,0:T(8,128)(2,1)} %param.20) | copy-start | bytes 3145732
  8.0 246.9 %all-gather.8.cloned.1.call-start = ((), (), s32[]{:S(2)}) async-start(), calls=%async_computation.11 | async-start | bytes 3145728 | tf_op jit(solution)/shard_map/all_gather | solution.py:249
  61.5 3.6 copy-start.23
  63.2 39.6 %copy-start.24 = (bf16[32,256]{1,0:T(8,128)(2,1)S(1)}, bf16[32,256]{1,0:T(8,128)(2,1)}, u32[]{:S(2)}) copy-start(bf16[32,256]{1,0:T(8,128)(2,1)} %param.24) | copy-start | bytes 49156
  63.2 78.6 %copy-start.25 = (bf16[32,256]{1,0:T(8,128)(2,1)S(1)}, bf16[32,256]{1,0:T(8,128)(2,1)}, u32[]{:S(2)}) copy-start(bf16[32,256]{1,0:T(8,128)(2,1)} %param.26) | copy-start | bytes 49156
  63.3 115.8 %copy-start.26 = (bf16[32,256]{1,0:T(8,128)(2,1)S(1)}, bf16[32,256]{1,0:T(8,128)(2,1)}, u32[]{:S(2)}) copy-start(bf16[32,256]{1,0:T(8,128)(2,1)} %param.25) | copy-start | bytes 49156
  63.3 154.4 %copy-start.27 = (bf16[256,32]{0,1:T(8,128)(2,1)S(1)}, bf16[256,32]{0,1:T(8,128)(2,1)}, u32[]{:S(2)}) copy-start(bf16[256,32]{0,1:T(8,128)(2,1)} %param.30) | copy-start | bytes 49156
  64.7 256.5 %reduce-scatter.12.cloned.1.call-start = ((), (), s32[]{:S(2)}) async-start(), calls=%async_computation.12 | async-start | bytes 3145728 | tf_op jit(solution)/shard_map/reduce_scatter | solution.py:278
  179.0 79.8 %copy-start.14 = (bf16[512,256]{1,0:T(8,128)(2,1)}, bf16[512,256]{1,0:T(8,128)(2,1)S(1)}, u32[]{:S(2)}) copy-start(bf16[512,256]{1,0:T(8,128)(2,1)S(1)} %all_gather.64) | copy-start | bytes 786436
  217.7 41.1 %copy-start.16 = (bf16[512,256]{1,0:T(8,128)(2,1)}, bf16[512,256]{1,0:T(8,128)(2,1)S(1)}, u32[]{:S(2)}) copy-start(bf16[512,256]{1,0:T(8,128)(2,1)S(1)} %all_gather.63) | copy-start | bytes 786436
  254.9 56.0 %copy-start.18 = (bf16[256,512]{0,1:T(8,128)(2,1)}, bf16[256,512]{0,1:T(8,128)(2,1)S(1)}, u32[]{:S(2)}) copy-start(bf16[256,512]{0,1:T(8,128)(2,1)S(1)} %all_gather.66) | copy-start | bytes 786436
  254.9 3.9 copy-start.4
  310.8 1.0 copy-start.13
  313.9 56.6 %all-gather.12.cloned.1.call-start = ((), (), s32[]{:S(2)}) async-start(), calls=%async_computation.14 | async-start | bytes 1114112 | tf_op jit(solution)/shard_map/all_gather | solution.py:209
  314.5 67.4 %all-gather.10.cloned.1.call-start = ((), (), s32[]{:S(2)}) async-start(), calls=%async_computation.13 | async-start | bytes 3145728 | tf_op jit(solution)/shard_map/all_gather | solution.py:292
  321.3 1.7 copy-start.1
  323.5 2.9 copy-start.28
  325.1 116.4 %all-gather.14.cloned.1.call-start = ((), (), s32[]{:S(2)}) async-start(), calls=%async_computation.15 | async-start | bytes 1114112 | tf_op jit(solution)/shard_map/all_gather | solution.py:211
  325.7 126.8 %all-gather.16.cloned.1.call-start = ((), (), s32[]{:S(2)}) async-start(), calls=%async_computation.17 | async-start | bytes 3145728 | tf_op jit(solution)/shard_map/all_gather | solution.py:309
  326.4 153.1 %reduce-scatter.16.cloned.1.call-start = ((), (), s32[]{:S(2)}) async-start(), calls=%async_computation.18 | async-start | bytes 3145728 | tf_op jit(solution)/shard_map/reduce_scatter | solution.py:318
  452.5 12.2 %copy-start.31 = (bf16[512,1024]{1,0:T(8,128)(2,1)S(1)}, bf16[512,1024]{1,0:T(8,128)(2,1)}, u32[]{:S(2)}) copy-start(bf16[512,1024]{1,0:T(8,128)(2,1)} %all-gather.12.cloned.1.call-done) | copy-start | bytes 3145732
  462.7 2.0 copy-start.32
  468.5 23.9 %reduce-scatter.14.cloned.1.call-start = ((), (), s32[]{:S(2)}) async-start(), calls=%async_computation.16 | async-start | bytes 3145728 | tf_op jit(solution)/shard_map/reduce_scatter | solution.py:297
  475.0 35.2 %all-gather.18.cloned.1.call-start = ((), (), s32[]{:S(2)}) async-start(), calls=%async_computation.19 | async-start | bytes 3145728 | tf_op jit(solution)/shard_map/all_gather | solution.py:330
  481.9 15.2 %copy-start.6 = (bf16[1024,512]{1,0:T(8,128)(2,1)S(1)}, bf16[1024,512]{1,0:T(8,128)(2,1)}, u32[]{:S(2)}) copy-start(bf16[1024,512]{1,0:T(8,128)(2,1)} %param.37) | copy-start | bytes 3145732
  495.8 1.3 copy-start.2
  497.1 13.1 %copy-start.19 = (bf16[256,512]{0,1:T(8,128)(2,1)S(1)}, bf16[256,512]{0,1:T(8,128)(2,1)}, u32[]{:S(2)}) copy-start(bf16[256,512]{0,1:T(8,128)(2,1)} %copy-done.18) | copy-start | bytes 786436
  498.4 115.2 %reduce-scatter.18.cloned.1.call-start = ((), (), s32[]{:S(2)}) async-start(), calls=%async_computation.20 | async-start | bytes 3145728 | tf_op jit(solution)/shard_map/reduce_scatter | solution.py:365
  510.2 2.5 copy-start.11
  571.4 1.8 copy-start.17
  573.2 1.0 copy-start.9
  573.2 2.0 copy-start.21
  573.2 2.6 copy-start.22
  576.3 1.0 copy-start.10
  576.3 2.0 copy-start.20
  577.3 2.1 copy-start.15
  578.4 1.0 copy-start.12
  581.5 1.6 copy-start.29
  581.5 120.0 %reduce-scatter.30.cloned.1.call-start = ((), (), s32[]{:S(2)}) async-start(), calls=%async_computation.26 | async-start | bytes 2228224 | tf_op jit(solution)/shard_map/reduce_scatter | solution.py:392
  588.9 1.7 copy-start.30
  588.9 168.2 %reduce-scatter.32.cloned.1.call-start = ((), (), s32[]{:S(2)}) async-start(), calls=%async_computation.27 | async-start | bytes 2228224 | tf_op jit(solution)/shard_map/reduce_scatter | solution.py:394
  596.8 3.9 copy-start.5
  596.8 236.9 %reduce-scatter.28.cloned.1.call-start = ((), (), s32[]{:S(2)}) async-start(), calls=%async_computation.25 | async-start | bytes 557056 | tf_op jit(solution)/shard_map/reduce_scatter | solution.py:389
  600.6 308.9 %reduce-scatter.20.cloned.1.call-start = ((), (), s32[]{:S(2)}) async-start(), calls=%async_computation.21 | async-start | bytes 557056 | tf_op jit(solution)/shard_map/reduce_scatter | solution.py:383
  603.5 381.7 %reduce-scatter.22.cloned.1.call-start = ((), (), s32[]{:S(2)}) async-start(), calls=%async_computation.22 | async-start | bytes 557056 | tf_op jit(solution)/shard_map/reduce_scatter | solution.py:384
  606.4 454.6 %reduce-scatter.24.cloned.1.call-start = ((), (), s32[]{:S(2)}) async-start(), calls=%async_computation.23 | async-start | bytes 557056 | tf_op jit(solution)/shard_map/reduce_scatter | solution.py:385
  609.3 527.4 %reduce-scatter.26.cloned.1.call-start = ((), (), s32[]{:S(2)}) async-start(), calls=%async_computation.24 | async-start | bytes 557056 | tf_op jit(solution)/shard_map/reduce_scatter | solution.py:386
  613.5 4.7 copy-start.3
  613.6 4.7 copy-start.7
  613.6 4.7 copy-start.8
Sparse Core Ops, SparseCore 0:
  64.8 6.4 all-gather.7
  314.0 7.1 reduce-scatter.11
  468.6 10.8 reduce-scatter.15
  481.6 10.7 reduce-scatter.13
Sparse Core Ops, SparseCore 1:
  317.5 52.9 all-gather.11
  372.6 9.3 all-gather.9
  384.9 56.5 all-gather.13
  443.2 9.3 all-gather.15
  498.5 11.6 all-gather.17
  581.6 10.7 reduce-scatter.17
  595.1 81.7 reduce-scatter.29
  679.6 77.5 reduce-scatter.31
  759.8 73.8 reduce-scatter.27
  836.6 72.9 reduce-scatter.19
  912.3 72.9 reduce-scatter.21
  988.1 72.8 reduce-scatter.23
  1063.7 72.9 reduce-scatter.25

commit v2 on v1

--- a/solution.py
+++ b/solution.py
@@ -12,6 +12,158 @@
 D = 512
 HEAD = 64
 L = 2048
+
+
+MESH = pl.DeviceIdType.MESH
+VECS = 128
+
+
+def peer_at(offset):
+    count = lax.axis_size("dp")
+    return lax.rem(lax.axis_index("dp") + offset, count)
+
+
+def greet_all(count):
+    barrier = pltpu.get_barrier_semaphore()
+
+    def greet(offset, carry):
+        pl.semaphore_signal(
+            barrier, inc=1, device_id={"dp": peer_at(offset)}, device_id_type=MESH
+        )
+        return carry
+
+    lax.fori_loop(1, count, greet, 0)
+    pl.semaphore_wait(barrier, count - 1)
+
+
+def gather_kernel(count, part_refs, whole_refs, send_sems, recv_sems, own_sems):
+    me = lax.axis_index("dp")
+
+    def copy_to(index, offset):
+        part, whole = part_refs[index], whole_refs[index]
+        rows = part.shape[0]
+        start = pl.multiple_of(me * rows, rows)
+        return pltpu.make_async_remote_copy(
+            src_ref=part,
+            dst_ref=whole.at[pl.ds(start, rows)],
+            send_sem=send_sems.at[index, offset - 1],
+            recv_sem=recv_sems.at[index, offset - 1],
+            device_id={"dp": peer_at(offset)},
+            device_id_type=MESH,
+        )
+
+    greet_all(count)
+    for index in range(len(part_refs)):
+
+        def begin(offset, carry):
+            copy_to(index, offset).start()
+            return carry
+
+        lax.fori_loop(1, count, begin, 0)
+    for index, (part, whole) in enumerate(zip(part_refs, whole_refs)):
+        rows = part.shape[0]
+        start = pl.multiple_of(me * rows, rows)
+        own = pltpu.make_async_copy(part, whole.at[pl.ds(start, rows)], own_sems.at[index])
+        own.start()
+        own.wait()
+
+        def finish(offset, carry):
+            copy_to(index, offset).wait()
+            return carry
+
+        lax.fori_loop(1, count, finish, 0)
+
+
+def gather_all(parts):
+    count = lax.axis_size("dp")
+    number = len(parts)
+
+    def body(*refs):
+        gather_kernel(count, refs[:number], refs[number : 2 * number], *refs[2 * number :])
+
+    return pl.pallas_call(
+        body,
+        in_specs=[pl.BlockSpec(memory_space=pltpu.VMEM)] * number,
+        out_specs=[pl.BlockSpec(memory_space=pltpu.VMEM)] * number,
+        out_shape=[
+            jax.ShapeDtypeStruct((count * part.shape[0], part.shape[1]), part.dtype)
+            for part in parts
+        ],
+        scratch_shapes=[
+            pltpu.SemaphoreType.DMA((number, count - 1)),
+            pltpu.SemaphoreType.DMA((number, count - 1)),
+            pltpu.SemaphoreType.DMA((number,)),
+        ],
+        compiler_params=pltpu.CompilerParams(collective_id=0, has_side_effects=True),
+    )(*parts)
+
+
+def scatter_kernel(count, whole_refs, out_refs, slot_refs, send_sems, recv_sems):
+    me = lax.axis_index("dp")
+
+    def copy_to(index, offset):
+        rows = out_refs[index].shape[0]
+        peer = peer_at(offset)
+        return pltpu.make_async_remote_copy(
+            src_ref=whole_refs[index].at[pl.ds(pl.multiple_of(peer * rows, rows), rows)],
+            dst_ref=slot_refs[index].at[offset - 1],
+            send_sem=send_sems.at[index, offset - 1],
+            recv_sem=recv_sems.at[index, offset - 1],
+            device_id={"dp": peer},
+            device_id_type=MESH,
+        )
+
+    greet_all(count)
+    for index in range(len(out_refs)):
+
+        def begin(offset, carry):
+            copy_to(index, offset).start()
+            return carry
+
+        lax.fori_loop(1, count, begin, 0)
+    for index, out in enumerate(out_refs):
+        rows = out.shape[0]
+        start = pl.multiple_of(me * rows, rows)
+        out[...] = whole_refs[index][pl.ds(start, rows), :].astype(jnp.float32)
+
+        def finish(offset, carry):
+            copy_to(index, offset).wait()
+            out[...] += slot_refs[index][offset - 1].astype(jnp.float32)
+            return carry
+
+        lax.fori_loop(1, count, finish, 0)
+
+
+def scatter_all(wholes):
+    count = lax.axis_size("dp")
+    number = len(wholes)
+
+    def body(*refs):
+        scatter_kernel(
+            count, refs[:number], refs[number : 2 * number], refs[2 * number : 3 * number],
+            *refs[3 * number :]
+        )
+
+    return pl.pallas_call(
+        body,
+        in_specs=[pl.BlockSpec(memory_space=pltpu.VMEM)] * number,
+        out_specs=[pl.BlockSpec(memory_space=pltpu.VMEM)] * number,
+        out_shape=[
+            jax.ShapeDtypeStruct((whole.shape[0] // count, whole.shape[1]), jnp.float32)
+            for whole in wholes
+        ],
+        scratch_shapes=[
+            pltpu.VMEM((count - 1, whole.shape[0] // count, whole.shape[1]), whole.dtype)
+            for whole in wholes
+        ]
+        + [
+            pltpu.SemaphoreType.DMA((number, count - 1)),
+            pltpu.SemaphoreType.DMA((number, count - 1)),
+        ],
+        compiler_params=pltpu.CompilerParams(
+            collective_id=1, has_side_effects=True, vmem_limit_bytes=40 * 1024 * 1024
+        ),
+    )(*wholes)
 
 
 def layer_norm(values, gain_vec, shift_vec):
@@ -194,40 +346,33 @@
     cotangent,
 ):
     member = lax.axis_index("tensor")
-    gathered = (
-        lax.all_gather(ln1_gain, "dp", axis=0, tiled=True),
-        lax.all_gather(ln1_bias, "dp", axis=0, tiled=True),
-        lax.all_gather(w_query, "dp", axis=0, tiled=True),
-        lax.all_gather(w_key, "dp", axis=0, tiled=True),
-        lax.all_gather(w_value, "dp", axis=0, tiled=True),
-        lax.all_gather(w_pos, "dp", axis=0, tiled=True),
-        lax.all_gather(bias_u, "dp", axis=0, tiled=True),
-        lax.all_gather(bias_w, "dp", axis=0, tiled=True),
-        lax.all_gather(w_out, "dp", axis=1, tiled=True),
-        lax.all_gather(ln2_gain, "dp", axis=0, tiled=True),
-        lax.all_gather(ln2_bias, "dp", axis=0, tiled=True),
-        lax.all_gather(w_up, "dp", axis=0, tiled=True),
-        lax.all_gather(bias_up, "dp", axis=0, tiled=True),
-        lax.all_gather(w_down, "dp", axis=1, tiled=True),
-        lax.all_gather(bias_down, "dp", axis=0, tiled=True),
-    )
-    (
-        gain_one,
-        shift_one,
-        query_mat,
-        key_mat,
-        value_mat,
-        pos_mat,
-        bias_one,
-        bias_two,
-        out_mat,
-        gain_two,
-        shift_two,
-        up_mat,
-        up_shift,
-        down_mat,
-        down_shift,
-    ) = gathered
+    shard_rows = w_query.shape[0]
+    direct = shard_rows % 16 == 0
+    squares = (w_query, w_key, w_value, w_pos, w_out.T)
+    wide = (w_up, w_down.T)
+    vectors = (ln1_gain, ln1_bias, bias_u, bias_w, ln2_gain, ln2_bias, bias_down)
+    if direct:
+        columns = jnp.stack(vectors, axis=1)
+        columns = jnp.pad(columns, ((0, 0), (0, VECS - len(vectors))))
+        up_row = jnp.pad(bias_up.reshape(1, -1), ((0, 15), (0, 0)))
+        near, far, up_rows = gather_all(
+            [jnp.concatenate(squares + (columns,), axis=1), jnp.concatenate(wide, axis=1), up_row]
+        )
+        near_mats = jnp.split(near[:, : -VECS], len(squares), axis=1)
+        far_mats = jnp.split(far, len(wide), axis=1)
+        vec_rows = near[:, -VECS:].T
+        full_vecs = [vec_rows[v] for v in range(len(vectors))]
+        up_shift = up_rows.reshape(-1, 16, up_rows.shape[1])[:, 0].reshape(-1)
+    else:
+        near_mats = [lax.all_gather(m, "dp", axis=0, tiled=True) for m in squares]
+        far_mats = [lax.all_gather(m, "dp", axis=0, tiled=True) for m in wide]
+        full_vecs = [lax.all_gather(v, "dp", axis=0, tiled=True) for v in vectors]
+        up_shift = lax.all_gather(bias_up, "dp", axis=0, tiled=True)
+    query_mat, key_mat, value_mat, pos_mat, out_back = near_mats
+    out_mat = out_back.T
+    up_mat, down_back = far_mats
+    down_mat = down_back.T
+    gain_one, shift_one, bias_one, bias_two, gain_two, shift_two, down_shift = full_vecs
     gain_one = gain_one.astype(jnp.float32)
     shift_one = shift_one.astype(jnp.float32)
     gain_two = gain_two.astype(jnp.float32)
@@ -377,45 +522,59 @@
     norm_back_one = jax.vjp(layer_norm, inputs, gain_one, shift_one)[1]
     grad_in_part, grad_gain_one, grad_shift_one = norm_back_one(grad_normed)
     grad_tokens = grad_residual + grad_in_part
-    shards = (
-        lax.psum_scatter(grad_gain_one, "dp", scatter_dimension=0, tiled=True),
-        lax.psum_scatter(grad_shift_one, "dp", scatter_dimension=0, tiled=True),
-        lax.psum_scatter(grad_query_mat, "dp", scatter_dimension=0, tiled=True),
-        lax.psum_scatter(grad_key_mat, "dp", scatter_dimension=0, tiled=True),
-        lax.psum_scatter(grad_value_mat, "dp", scatter_dimension=0, tiled=True),
-        lax.psum_scatter(grad_pos, "dp", scatter_dimension=0, tiled=True),
-        lax.psum_scatter(grad_bias_one, "dp", scatter_dimension=0, tiled=True),
-        lax.psum_scatter(grad_bias_two, "dp", scatter_dimension=0, tiled=True),
-        lax.psum_scatter(grad_out_mat, "dp", scatter_dimension=1, tiled=True),
-        lax.psum_scatter(ffn_terms[0], "dp", scatter_dimension=0, tiled=True),
-        lax.psum_scatter(ffn_terms[1], "dp", scatter_dimension=0, tiled=True),
-        lax.psum_scatter(ffn_terms[2], "dp", scatter_dimension=0, tiled=True),
-        lax.psum_scatter(ffn_terms[3], "dp", scatter_dimension=0, tiled=True),
-        lax.psum_scatter(ffn_terms[4], "dp", scatter_dimension=1, tiled=True),
-        lax.psum_scatter(ffn_terms[5], "dp", scatter_dimension=0, tiled=True),
-    )
-    summed = lax.psum(
-        (shards[0], shards[1], shards[6], shards[7], shards[9], shards[10], shards[12], shards[14]),
-        "tensor",
-    )
+    grad_squares = (grad_query_mat, grad_key_mat, grad_value_mat, grad_pos, grad_out_mat.T)
+    grad_wides = (grad_up, grad_down.T)
+    grad_vecs = jnp.stack(
+        (
+            grad_gain_one, grad_shift_one, grad_bias_one, grad_bias_two,
+            ffn_terms[0], ffn_terms[1], ffn_terms[5],
+        )
+    )
+    grad_vecs, grad_up_row = lax.psum((grad_vecs, ffn_terms[3]), "tensor")
+    if direct:
+        bf16 = jnp.bfloat16
+        columns = jnp.pad(grad_vecs.T, ((0, 0), (0, VECS - grad_vecs.shape[0]))).astype(bf16)
+        pieces = D // shard_rows
+        up_rows = jnp.pad(grad_up_row.reshape(pieces, 1, -1), ((0, 0), (0, 15), (0, 0)))
+        near, far, up_rows = scatter_all(
+            [
+                jnp.concatenate([m.astype(bf16) for m in grad_squares] + [columns], axis=1),
+                jnp.concatenate([m.astype(bf16) for m in grad_wides], axis=1),
+                up_rows.reshape(pieces * 16, -1).astype(bf16),
+            ]
+        )
+        squares = jnp.split(near[:, :-VECS], len(grad_squares), axis=1)
+        wides = jnp.split(far, 2, axis=1)
+        vec_rows = near[:, -VECS:].T
+        vecs = [vec_rows[v] for v in range(grad_vecs.shape[0])]
+        up_part = up_rows[0]
+    else:
+
+        def share(array):
+            return lax.psum_scatter(array, "dp", scatter_dimension=0, tiled=True)
+
+        squares = [share(m) for m in grad_squares]
+        wides = [share(m) for m in grad_wides]
+        vecs = [share(v) for v in grad_vecs]
+        up_part = share(grad_up_row)
     return (
         output.astype(jnp.bfloat16),
         grad_tokens,
-        summed[0],
-        summed[1],
-        shards[2],
-        shards[3],
-        shards[4],
-        shards[5],
-        summed[2],
-        summed[3],
-        shards[8],
-        summed[4],
-        summed[5],
-        shards[11],
-        summed[6],
-        shards[13],
-        summed[7],
+        vecs[0],
+        vecs[1],
+        squares[0],
+        squares[1],
+        squares[2],
+        squares[3],
+        vecs[2],
+        vecs[3],
+        squares[4].T,
+        vecs[4],
+        vecs[5],
+        wides[0],
+        up_part,
+        wides[1].T,
+        vecs[6],
     )
 
 

time: 1150 us -> 489 us (0.43)
  waiting for transfers between devices: 545 us -> 58.2 us
  blocking collectives: 354 us -> 5.45 us
  Pallas kernels: 100 us -> 280 us
    reduce_scatter x7 -> x0, waiting for transfers between devices: 435 us -> none  [the longest x1 76.6 us: local(): lax.psum_scatter(grad_out_mat, 'dp', scatter_dimension=1, tiled=True)]
    all_gather x6 -> x0, blocking collectives: 230 us -> none  [the longest x1 40.7 us: local(): lax.all_gather(bias_up, 'dp', axis=0, tiled=True)]
    pallas_call x0 -> x2, Pallas kernels: none -> 180 us  [the longest x1 91.5 us: gather_all(): pl.pallas_call(body, in_specs=[pl.BlockSpec(memory_space=pltpu.VMEM)] * n...]
    unnamed x2 -> x0, blocking collectives: 121 us -> none
    all_gather x2 -> x0, waiting for transfers between devices: 52.6 us -> none  [the longest x1 49.2 us: local(): lax.all_gather(w_down, 'dp', axis=1, tiled=True)]
  transfers between devices with their start and end apart: 17 -> 8, of which waited for: 14 -> 7; matrix products, arithmetic and copies ran while one was open for 5% -> 8% of each run, Pallas kernels for 0% -> 0%
where the time goes in v2:
time: 489 us; the launch traced here: 484 us
  Pallas kernels  280 us (57%)
  matrix products  59 us (12%)
  waiting for transfers between devices  58.2 us (12%)
  other arithmetic  37 us (8%)
  local copies, waits for them, and re-layouts  28.5 us (6%)
  between operations  14.9 us (3%)
  blocking collectives  5.45 us (1%)
    pallas_call x1, Pallas kernels, gather_all(): pl.pallas_call(body, in_specs=[pl.BlockSpec(memory_space=pltpu.VMEM)] * n...  91.5 us
    pallas_call x1, Pallas kernels, scatter_all(): pl.pallas_call(body, in_specs=[pl.BlockSpec(memory_space=pltpu.VMEM)] * n...  88.1 us
    pallas_call x1, Pallas kernels, attend_back_all(): pl.pallas_call(attend_back_kernel, grid=(heads,), in_specs=[per_head(TILE...  55.7 us
    pallas_call x1, Pallas kernels, attend_all(): pl.pallas_call(attend_kernel, grid=(heads,), in_specs=[per_head(HEAD, L)]...  44.7 us
    dot_general x9, matrix products, times_transpose(): lax.dot_general(left, right, (((1,), (1,)), ((), ())), preferred_element_...  24.9 us
    unnamed x77, local copies, waits for them, and re-layouts  14.5 us
    all_gather x1, waiting for transfers between devices, local(): lax.all_gather(grad_residual.astype(jnp.bfloat16), 'tensor', axis=0, tile...  11.8 us
    reduce_scatter x1, waiting for transfers between devices, local(): lax.psum_scatter(contract_rows(take_cols(mixed_cols, jnp.int32(0), own_ro...  10.9 us
  transfers between devices with their start and end apart: 8, of which 7 were waited for; matrix products, arithmetic and copies ran while one was open for 8% of the time, Pallas kernels for 0%

profile of v2, /device:TPU:0, one launch (start us, length us, event | category | flops | bytes accessed | tf_op | source)
XLA Modules:
  0.0 483.7 jit_solution(7166178037732844576)
XLA Ops:
  7.2 0.8 constant_dynamic-update-slice_fusion.5
  8.0 0.8 stack.49
  11.8 1.6 pad_maximum_fusion.1.refs_1_
  13.4 1.3 pad.19.refs_2_
  14.7 91.5 %shard_map.323 = (bf16[512,1408]{1,0:T(8,128)(2,1)}, bf16[512,2048]{1,0:T(8,128)(2,1)}, bf16[256,128]{1,0:T(8,128)(2,1)}) custom-call(bf16[32,1408]{1,0:T(8,128)(2,1)} %copy-done.26, bf16[32,2048]{1,0:T(8,128)(2,1)} %pad_maximum_fusion.1.refs_1_, bf16[16,128]{1,0:T(8,128)(2,1)} %pad.19.refs_2_), custom_call_target="tpu_custom_call" | custom-call | tf_op jit(solution)/shard_map/pallas_call | solution.py:84
  106.2 0.9 slice_bitcast_fusion.2
  108.4 1.4 fusion.19
  110.1 0.8 copy.76
  111.2 7.6 %all-gather.5.cloned.1.call-done = bf16[2048,512]{1,0:T(8,128)(2,1)} async-done(((bf16[1024,512]{1,0:T(8,128)(2,1)}), bf16[2048,512]{1,0:T(8,128)(2,1)}) %all-gather.5.cloned.1.call-update) | async-done | bytes 2097168 | tf_op jit(solution)/shard_map/all_gather | solution.py:394
  118.8 2.5 convolution_convert_fusion.4
  121.3 1.4 maximum_maximum_fusion.value_ref
  122.7 1.7 convolution_convert_fusion.5
  124.5 3.1 add_convert_fusion.4
  127.5 44.7 %shard_map.324 = (bf16[4,256,11008]{2,1,0:T(8,128)(2,1)}, f32[4,80,2048]{2,1,0:T(8,128)}) custom-call(bf16[4,64,2048]{2,1,0:T(8,128)(2,1)} %bitcast.114, bf16[4,64,2048]{2,1,0:T(8,128)(2,1)} %bitcast.113, bf16[4,64,2048]{2,1,0:T(8,128)(2,1)} %bitcast.101, bf16[4,80,2048]{2,1,0:T(8,128)(2,1)} %maximum_maximum_fusion.value_ref, bf16[4,64,512]{2,1,0:T(8,128)(2,1)} %bitcast.116, ...), custom_call_target="tpu_custom_call" | custom-call | tf_op jit(solution)/shard_map/pallas_call | solution.py:294
  172.2 1.0 broadcast_multiply_fusion
  173.2 1.8 fusion.27
  175.0 1.0 copy-done.17
  176.0 2.1 convolution_convert_fusion.2
  178.2 10.9 %reduce-scatter.5.cloned.1.call-done = bf16[1024,512]{1,0:T(8,128)(2,1)} async-done(((bf16[2048,512]{1,0:T(8,128)(2,1)}), bf16[1024,512]{1,0:T(8,128)(2,1)}) %reduce-scatter.5.cloned.1.call-update) | async-done | bytes 1048592 | tf_op jit(solution)/shard_map/reduce_scatter | solution.py:423
  189.1 1.7 fusion.29
  191.3 1.5 add_convert_fusion.3
  193.9 0.8 slice_convert_fusion
  194.7 10.1 %all-gather.7.cloned.1.call-done = bf16[2048,512]{1,0:T(8,128)(2,1)} async-done(((bf16[1024,512]{1,0:T(8,128)(2,1)}), bf16[2048,512]{1,0:T(8,128)(2,1)}) %all-gather.7.cloned.1.call-update) | async-done | bytes 2097168 | tf_op jit(solution)/shard_map/all_gather | solution.py:437
  204.8 10.7 %multiply_convert_fusion = (bf16[2048,1024]{1,0:T(8,128)(2,1)}, f32[2048,1024]{1,0:T(8,128)}) fusion(f32[1024]{0:T(1024)S(1)} %dynamic_slice.17, bf16[2048,512]{1,0:T(8,128)(2,1)} %all-gather.7.cloned.1.call-done, bf16[512,2048]{1,0:T(8,128)(2,1)} %get-tuple-element.32), kind=kOutput, calls=%fused_computation.15 | convolution fusion | flops 2168455168 | bytes 15732736 | tf_op jit(solution)/shard_map/dot_general | solution.py:438
  215.5 2.5 all-gather.9.cloned.1.call-done
  218.0 10.9 %convert_reduce_fusion = (f32[1024]{0:T(1024)S(1)}, bf16[2048,1024]{1,0:T(8,128)(2,1)S(1)}) fusion(f32[2048,1024]{1,0:T(8,128)} %get-tuple-element.93, f32[1024]{0:T(1024)S(1)} %dynamic_slice.17, bf16[2048,512]{1,0:T(8,128)(2,1)} %all-gather.9.cloned.1.call-done, bf16[512,2048]{1,0:T(8,128)(2,1)} %get-tuple-element.32), kind=kOutput, calls=%fused_computation.14 | convolution fusion | flops 2195717120 | bytes 15736832 | tf_op jit(solution)/shard_map/dot_general | solution.py:190
  228.9 2.0 copy-done.32
  231.0 3.8 convolution_convert_fusion
  234.8 6.2 %convolution_convert_fusion.1 = bf16[2048,512]{1,0:T(8,128)(2,1)} fusion(bf16[2048,1024]{1,0:T(8,128)(2,1)} %get-tuple-element.92, bf16[512,2048]{1,0:T(8,128)(2,1)} %get-tuple-element.32), kind=kOutput, calls=%fused_computation.33 | convolution fusion | flops 2148532224 | bytes 7340032 | tf_op jit(solution)/shard_map/dot_general | solution.py:443
  241.1 4.6 reduce-scatter.9.cloned.1.call-done
  245.7 3.0 fusion.25
  248.7 9.9 %reduce-scatter.7.cloned.1.call-done = bf16[1024,512]{1,0:T(8,128)(2,1)} async-done(((bf16[2048,512]{1,0:T(8,128)(2,1)}), bf16[1024,512]{1,0:T(8,128)(2,1)}) %reduce-scatter.7.cloned.1.call-update) | async-done | bytes 1048592 | tf_op jit(solution)/shard_map/reduce_scatter | solution.py:442
  258.6 3.3 fusion.56
  262.0 1.3 copy-done.3
  263.3 1.3 fusion.32
  264.7 11.8 %all-gather.11.cloned.1.call-done = bf16[2048,512]{1,0:T(8,128)(2,1)} async-done(((bf16[1024,512]{1,0:T(8,128)(2,1)}), bf16[2048,512]{1,0:T(8,128)(2,1)}) %all-gather.11.cloned.1.call-update) | async-done | bytes 2097168 | tf_op jit(solution)/shard_map/all_gather | solution.py:475
  276.5 2.5 convolution_convert_fusion.3
  279.0 1.6 multiply_reduce_fusion
  280.6 1.4 maximum_maximum_fusion.1.aug_ref
  282.1 55.7 %shard_map.325 = (f32[4,64,2048]{2,1,0:T(8,128)}, f32[4,64,2048]{2,1,0:T(8,128)}, f32[4,64,2048]{2,1,0:T(8,128)}, f32[4,64,2048]{2,1,0:T(8,128)}, f32[4,64,512]{2,1,0:T(8,128)}) custom-call(bf16[4,256,11008]{2,1,0:T(8,128)(2,1)} %get-tuple-element.34.e_ref, bf16[4,64,2048]{2,1,0:T(8,128)(2,1)} %bitcast.112, bf16[4,64,2048]{2,1,0:T(8,128)(2,1)} %bitcast.111, ...), custom_call_target="tpu_custom_call" | custom-call | tf_op jit(solution)/shard_map/pallas_call | solution.py:311
  337.8 1.8 convert_element_type.251
  339.8 0.8 fusion.46
  340.7 1.0 copy-done.21
  342.8 0.8 fusion.49
  343.8 1.0 copy-done.20
  344.9 1.0 copy-done.15
  345.9 2.1 add_convert_fusion
  348.6 1.6 dynamic_update_slice.13
  350.3 4.7 convolution_convert_fusion.7
  355.0 2.4 fusion.30
  358.5 0.8 copy.81
  360.5 2.6 fusion.33
  363.1 0.7 fusion.34
  364.4 0.7 fusion.35
  366.4 0.8 fusion.36
  367.2 3.1 convert_reduce_fusion.1
  371.0 3.0 fusion.26
  374.0 3.8 convert_reduce_fusion.4
  377.8 0.8 stack.54
  378.6 0.8 copy.83
  379.4 5.4 %all-reduce.4 = (bf16[7,512]{0,1:T(8,128)(2,1)}, bf16[2048]{0:T(1024)(128)(2,1)S(1)}) all-reduce(f32[7,512]{0,1:T(8,128)} %copy.83, f32[2048]{0:T(1024)} %dynamic_update_slice.13), channel_id=1, replica_groups=mesh['dp'=16,'tensor'=2] {'tensor'}, use_global_device_ids=true, to_apply=%region_20.21 | all-reduce | flops 5632 | bytes 33792 | tf_op jit(solution)/shard_map/psum | solution.py:533
  384.9 1.0 pad_dynamic-update-slice_fusion.refs_0_
  385.9 88.1 %shard_map.326 = (f32[32,1408]{1,0:T(8,128)S(1)}, f32[32,2048]{1,0:T(8,128)S(1)}, f32[16,128]{1,0:T(8,128)S(1)}) custom-call(bf16[512,1408]{1,0:T(8,128)(2,1)S(1)} %pad_dynamic-update-slice_fusion.refs_0_, bf16[512,2048]{1,0:T(8,128)(2,1)S(1)} %pad_maximum_fusion.refs_1_, bf16[256,128]{1,0:T(8,128)(2,1)S(1)} %bitcast.100), custom_call_target="tpu_custom_call" | custom-call | tf_op jit(solution)/shard_map/pallas_call | solution.py:147
  475.3 0.8 slice_reduce_fusion
  (128 shorter events, 15.6 us)
Async XLA Ops:
  7.2 100.4 %copy-start = (bf16[1024,512]{1,0:T(8,128)(2,1)S(1)}, bf16[1024,512]{1,0:T(8,128)(2,1)}, u32[]{:S(2)}) copy-start(bf16[1024,512]{1,0:T(8,128)(2,1)} %param.20) | copy-start | bytes 3145732
  7.2 111.6 %all-gather.5.cloned.1.call-start = ((), (), s32[]{:S(2)}) async-start(), calls=%async_computation.4 | async-start | bytes 3145728 | tf_op jit(solution)/shard_map/all_gather | solution.py:394
  11.8 2.8 copy-start.26
  107.8 2.2 copy-start.13
  108.3 1.6 copy-start.27
  109.8 79.3 %reduce-scatter.5.cloned.1.call-start = ((), (), s32[]{:S(2)}) async-start(), calls=%async_computation.5 | async-start | bytes 3145728 | tf_op jit(solution)/shard_map/reduce_scatter | solution.py:423
  118.8 3.9 copy-start.5
  175.0 1.0 copy-start.17
  178.1 26.7 %all-gather.7.cloned.1.call-start = ((), (), s32[]{:S(2)}) async-start(), calls=%async_computation.6 | async-start | bytes 3145728 | tf_op jit(solution)/shard_map/all_gather | solution.py:437
  189.1 1.7 copy-start.2
  192.9 25.2 %all-gather.9.cloned.1.call-start = ((), (), s32[]{:S(2)}) async-start(), calls=%async_computation.8 | async-start | bytes 3145728 | tf_op jit(solution)/shard_map/all_gather | solution.py:454
  193.4 52.3 %reduce-scatter.9.cloned.1.call-start = ((), (), s32[]{:S(2)}) async-start(), calls=%async_computation.9 | async-start | bytes 3145728 | tf_op jit(solution)/shard_map/reduce_scatter | solution.py:463
  218.0 12.9 %copy-start.31 = (bf16[512,2048]{1,0:T(8,128)(2,1)S(1)}, bf16[512,2048]{1,0:T(8,128)(2,1)}, u32[]{:S(2)}) copy-start(bf16[512,2048]{1,0:T(8,128)(2,1)} %get-tuple-element.32) | copy-start | bytes 6291460
  228.9 2.0 copy-start.32
  234.8 23.9 %reduce-scatter.7.cloned.1.call-start = ((), (), s32[]{:S(2)}) async-start(), calls=%async_computation.7 | async-start | bytes 3145728 | tf_op jit(solution)/shard_map/reduce_scatter | solution.py:442
  241.0 35.5 %all-gather.11.cloned.1.call-start = ((), (), s32[]{:S(2)}) async-start(), calls=%async_computation.10 | async-start | bytes 3145728 | tf_op jit(solution)/shard_map/all_gather | solution.py:475
  245.7 12.9 %copy-start.19 = (bf16[1024,512]{1,0:T(8,128)(2,1)S(1)}, bf16[1024,512]{1,0:T(8,128)(2,1)}, u32[]{:S(2)}) copy-start(bf16[1024,512]{1,0:T(8,128)(2,1)} %reduce-scatter.9.cloned.1.call-done) | copy-start | bytes 3145732
  258.6 4.6 copy-start.7
  262.0 1.3 copy-start.3
  264.6 14.4 %copy-start.12 = (f32[4,80,2048]{2,1,0:T(8,128)S(1)}, f32[4,80,2048]{2,1,0:T(8,128)}, u32[]{:S(2)}) copy-start(f32[4,80,2048]{2,1,0:T(8,128)} %get-tuple-element.31) | copy-start | bytes 7864324
  264.6 102.6 %reduce-scatter.11.cloned.1.call-start = ((), (), s32[]{:S(2)}) async-start(), calls=%async_computation.11 | async-start | bytes 3145728 | tf_op jit(solution)/shard_map/reduce_scatter | solution.py:510
  337.8 2.0 copy-start.14
  339.7 1.0 copy-start.9
  339.8 1.8 copy-start.21
  339.8 2.5 copy-start.22
  342.8 1.0 copy-start.11
  342.8 2.0 copy-start.20
  344.9 1.0 copy-start.15
  347.9 2.3 copy-start.29
  350.2 4.7 copy-start.30
  350.2 4.7 copy-start.33
  357.4 1.1 copy-start.25
  359.3 3.8 copy-start.6
  359.3 3.8 copy-start.10
  359.4 0.6 copy-start.28
  363.1 1.2 copy-start.16
  364.4 0.9 copy-start.24
  364.4 1.3 copy-start.18
  364.4 2.0 copy-start.23
  367.2 3.9 copy-start.1
  367.2 6.8 %copy-start.4 = (f32[1024,512]{1,0:T(8,128)S(1)}, f32[1024,512]{1,0:T(8,128)}, u32[]{:S(2)}) copy-start(f32[1024,512]{1,0:T(8,128)} %copy-done.3) | copy-start | bytes 6291460
  367.2 6.8 %copy-start.8 = (bf16[1024,512]{1,0:T(8,128)(2,1)S(1)}, bf16[1024,512]{1,0:T(8,128)(2,1)}, u32[]{:S(2)}) copy-start(bf16[1024,512]{1,0:T(8,128)(2,1)} %param.37) | copy-start | bytes 3145732
Sparse Core Ops, SparseCore 0:
  109.9 8.7 all-gather.4
  178.2 10.7 reduce-scatter.4
  193.0 11.7 all-gather.6
  206.2 11.7 all-gather.8
  234.9 10.7 reduce-scatter.8
  247.8 10.7 reduce-scatter.6
  264.7 11.7 all-gather.10
  348.1 10.7 reduce-scatter.10
